TPU v7x, 32 devices: a whole 2x2x4 slice. The times are simulated.
32 devices in a mesh: grp: 2 (over x), fsdp: 8 (over z, y), tp: 2 (over core).
Axes of the slice: x: 2, y: 2, z: 4, core: 2. Of those that a mesh axis runs over, the one named last changes fastest.
Arguments:
- hidden: bfloat16 [256, 2, 5120], P('grp', None, 'fsdp'), parts along dimension 0, may hold values from -90 to 90
- input_gain: float32 [5120], P('fsdp'), may hold values from 0.3 to 3
- q_gain: float32 [128], replicated, may hold values from 0.5 to 2.5
- k_gain: float32 [128], replicated, may hold values from 0.5 to 2.5
- base_qkv: bfloat16 [10240, 5120], P('tp', 'fsdp'), may hold values from -0.078125 to 0.078125
- codes_qkv: bfloat16 [10240, 5120], P(('tp', 'fsdp')), may hold values from -448 to 448
- scale_qkv: float32 [80, 40], replicated, may hold values from 2e-05 to 0.0002
- base_out: bfloat16 [5120, 8192], P('fsdp', 'tp'), may hold values from -0.125 to 0.125
- codes_out: bfloat16 [5120, 8192], P(('fsdp', 'tp')), may hold values from -448 to 448
- scale_out: float32 [40, 64], replicated, may hold values from 2e-05 to 0.0002
- lengths: int32 [256], P(('grp', 'fsdp')), parts along dimension 0, may hold values from 1 to 512, as said below
- key_cache: bfloat16 [256, 512, 8, 128], P(('grp', 'fsdp'), None, 'tp'), parts along dimension 0, may hold values from -2.5 to 2.5
- value_cache: bfloat16 [256, 512, 8, 128], P(('grp', 'fsdp'), None, 'tp'), parts along dimension 0, may hold values from -2.5 to 2.5
Outputs:
- decoded: bfloat16 [256, 2, 5120], P('grp', None, 'fsdp'), parts along dimension 0
There are 2 independent parts, one for each index of `grp`. A program takes and returns all parts, laid end to end along the dimension named above; an argument that names none is the same for every part. Nothing has to cross between parts.
Inputs may be any that keep to these rules, and one draw needn't show every extreme that they name: Keys and values of a row at positions of lengths or more are not read; some row has exactly 512.
All inputs are finite; a program needn't handle non-finite values.
Results may differ from a plain program's by a relative error of at most 0.005.
The roundings to bfloat16 on the way count: a program that leaves them out, or rounds other values in their place, can miss the bound.
Values may be sent and summed in bfloat16 or wider, within the bound.
A program may use at most 192 MiB of HBM per device.

v0:
```python
import math

import jax
import jax.numpy as jnp
from jax import lax
from jax.sharding import PartitionSpec as P

D = 5120
BLOCK = 128


epsilon = 1e-06
rope_base = 1000000.0


def head_norm(values, gain):
    return values * lax.rsqrt(jnp.mean(values * values, axis=-1, keepdims=True) + epsilon) * gain


def rotate(values, positions):
    half_dim = values.shape[-1] // 2
    frequency = jnp.exp(
        jnp.arange(half_dim).astype(jnp.float32) * (-2.0 * math.log(rope_base) / values.shape[-1])
    )
    angles = positions.astype(jnp.float32)[..., None] * frequency
    angles = angles.reshape(
        positions.shape + (1,) * (values.ndim - positions.ndim - 1) + (half_dim,)
    )
    cosine = jnp.cos(angles)
    sine_part = jnp.sin(angles)
    first_part = values[..., :half_dim]
    second_part = values[..., half_dim:]
    return jnp.concatenate(
        [
            first_part * cosine - second_part * sine_part,
            second_part * cosine + first_part * sine_part,
        ],
        axis=-1,
    )


def attend(projected, lengths, key_cache, value_cache, q_gain, k_gain):
    row_count = projected.shape[0]
    groups = key_cache.shape[2]
    head_dim = key_cache.shape[3]
    grouped = projected.reshape(row_count, 2, groups, -1, head_dim)
    per_group = grouped.shape[3]
    queries = grouped[:, :, :, : per_group - 2]
    new_keys = grouped[:, :, :, per_group - 2]
    new_values = grouped[:, :, :, per_group - 1].astype(jnp.bfloat16)
    positions = lengths[:, None] + jnp.arange(2, dtype=jnp.int32)[None, :]
    queries = rotate(head_norm(queries, q_gain), positions).astype(jnp.bfloat16)
    new_keys = rotate(head_norm(new_keys, k_gain), positions).astype(jnp.bfloat16)
    scaling = 1.0 / math.sqrt(head_dim)
    cache_scores = (
        jnp.einsum("rsgqd,rlgd->rsgql", queries, key_cache, preferred_element_type=jnp.float32)
        * scaling
    )
    new_scores = (
        jnp.einsum("rsgqd,rtgd->rsgqt", queries, new_keys, preferred_element_type=jnp.float32)
        * scaling
    )
    cache_mask = (
        jnp.arange(key_cache.shape[1], dtype=jnp.int32)[None, :] < lengths[:, None]
    ).reshape(row_count, 1, 1, 1, -1)
    step_mask = (
        jnp.arange(2, dtype=jnp.int32)[None, :] <= jnp.arange(2, dtype=jnp.int32)[:, None]
    ).reshape(1, 2, 1, 1, 2)
    cache_weights = jnp.where(cache_mask, jnp.exp(cache_scores), 0.0)
    new_weights = jnp.where(step_mask, jnp.exp(new_scores), 0.0)
    totals = jnp.sum(cache_weights, axis=-1) + jnp.sum(new_weights, axis=-1)
    cache_weights = (cache_weights / totals[..., None]).astype(jnp.bfloat16)
    new_weights = (new_weights / totals[..., None]).astype(jnp.bfloat16)
    mixed = jnp.einsum(
        "rsgql,rlgd->rsgqd", cache_weights, value_cache, preferred_element_type=jnp.float32
    )
    mixed = mixed + jnp.einsum(
        "rsgqt,rtgd->rsgqd", new_weights, new_values, preferred_element_type=jnp.float32
    )
    return mixed.reshape(row_count, 2, -1).astype(jnp.bfloat16)


def on_device(
    hidden,
    input_gain,
    q_gain,
    k_gain,
    base_qkv,
    codes_qkv,
    scale_qkv,
    base_out,
    codes_out,
    scale_out,
    lengths,
    key_cache,
    value_cache,
):
    fsdp_index = lax.axis_index("fsdp")
    tp_index = lax.axis_index("tp")
    qkv_rows, width_part = base_qkv.shape
    arrived_out = lax.all_to_all(codes_out, "tp", split_axis=1, concat_axis=0, tiled=True)
    out_rows, out_columns = base_out.shape
    column_blocks = out_columns // BLOCK
    scale_columns = lax.dynamic_slice_in_dim(scale_out, tp_index * column_blocks, column_blocks, 1)
    row_ids = (fsdp_index * out_rows + jnp.arange(out_rows, dtype=jnp.int32)) // BLOCK
    row_pick = (
        row_ids[:, None] == jnp.arange(scale_out.shape[0], dtype=jnp.int32)[None, :]
    ).astype(jnp.float32)
    row_scale = jnp.dot(row_pick, scale_columns, precision=lax.Precision.HIGHEST)
    delta_out = (
        arrived_out.astype(jnp.float32).reshape(out_rows, column_blocks, BLOCK)
        * row_scale[:, :, None]
    )
    new_out = (base_out.astype(jnp.float32) + delta_out.reshape(out_rows, out_columns)).astype(
        jnp.bfloat16
    )
    hidden_float = hidden.astype(jnp.float32)
    square_part = jnp.sum(hidden_float * hidden_float, axis=-1)
    mean_square = lax.psum(square_part, "fsdp") / D
    normed = (hidden_float * lax.rsqrt(mean_square + epsilon)[..., None] * input_gain).astype(
        jnp.bfloat16
    )
    arrived = lax.all_to_all(codes_qkv, "fsdp", split_axis=1, concat_axis=0, tiled=True)
    row_blocks = qkv_rows // BLOCK
    scale_rows = lax.dynamic_slice_in_dim(scale_qkv, tp_index * row_blocks, row_blocks, 0)
    column_ids = (fsdp_index * width_part + jnp.arange(width_part, dtype=jnp.int32)) // BLOCK
    column_pick = (
        jnp.arange(scale_qkv.shape[1], dtype=jnp.int32)[:, None] == column_ids[None, :]
    ).astype(jnp.float32)
    column_scale = jnp.dot(scale_rows, column_pick, precision=lax.Precision.HIGHEST)
    delta_part = (
        arrived.astype(jnp.float32).reshape(row_blocks, BLOCK, width_part)
        * column_scale[:, None, :]
    )
    new_qkv = (base_qkv.astype(jnp.float32) + delta_part.reshape(qkv_rows, width_part)).astype(
        jnp.bfloat16
    )
    projected = lax.psum_scatter(
        lax.dot_general(
            normed, new_qkv, (((2,), (1,)), ((), ())), preferred_element_type=jnp.float32
        ),
        "fsdp",
        scatter_dimension=0,
        tiled=True,
    )
    attended = attend(projected, lengths, key_cache, value_cache, q_gain, k_gain)
    partial_out = lax.dot_general(
        lax.all_gather(attended, "fsdp", axis=0, tiled=True),
        new_out,
        (((2,), (1,)), ((), ())),
        preferred_element_type=jnp.float32,
    )
    return lax.psum(partial_out, "tp").astype(jnp.bfloat16)


def solution(mesh):
    return jax.shard_map(
        on_device,
        mesh=mesh,
        in_specs=(
            P("grp", None, "fsdp"),
            P("fsdp"),
            P(),
            P(),
            P("tp", "fsdp"),
            P(("tp", "fsdp"), None),
            P(),
            P("fsdp", "tp"),
            P(("fsdp", "tp"), None),
            P(),
            P(("grp", "fsdp")),
            P(("grp", "fsdp"), None, "tp", None),
            P(("grp", "fsdp"), None, "tp", None),
        ),
        out_specs=P("grp", None, "fsdp"),
        check_vma=False,
    )
```

profile of v0, /device:TPU:0, one launch (start us, length us, event | category | flops | bytes accessed | tf_op | source)
XLA Modules:
  0.0 385.4 jit_solution(13681365693499221171)
XLA Ops:
  6.5 0.0 copy-start
  6.5 9.5 %copy.73 = bf16[640,5120]{0,1:T(8,128)(2,1)} copy(bf16[640,5120]{1,0:T(8,128)(2,1)} %param.18) | data formatting | bytes 13107200 | tf_op args[5]
  16.0 9.5 %copy.74 = bf16[640,8,640]{2,0,1:T(8,128)(2,1)} copy(bf16[640,8,640]{0,2,1:T(8,128)(2,1)} %bitcast.79) | data formatting | bytes 13107200 | tf_op jit(solution)/shard_map/all_to_all | solution.py:123
  25.5 0.0 copy-start.2
  25.5 0.0 copy-start.4
  25.5 7.4 %all-to-all-start = ((bf16[640,8,640]{2,0,1:T(8,128)(2,1)}), bf16[640,8,640]{2,0,1:T(8,128)(2,1)}, u32[]{:S(2)}, u32[]{:S(2)}) async-start(bf16[640,8,640]{2,0,1:T(8,128)(2,1)} %copy.74), calls=%async_computation | async-start | bytes 13107200 | tf_op jit(solution)/shard_map/all_to_all | solution.py:123
  32.9 0.0 reduce-scatter.2.cloned.1.call-start
  33.0 0.0 copy-done.2
  33.0 0.4 fusion.26
  33.4 0.1 copy.71
  33.4 128.9 %psum.14 = f32[128,2]{0,1:T(2,128)S(1)} all-reduce(f32[128,2]{0,1:T(2,128)S(1)} %copy.71), channel_id=1, replica_groups=mesh['grp'=2,'fsdp'=8,'tp'=2] {'fsdp'}, use_global_device_ids=true, to_apply=%region_1.2 | all-reduce | flops 256 | bytes 2048 | tf_op jit(solution)/shard_map/psum | solution.py:119
  162.4 0.1 copy.72
  162.5 0.0 copy-done
  162.5 0.3 fusion.32
  162.8 0.0 copy-done.4
  162.9 0.4 fusion.28
  163.3 13.6 %all-to-all-done = bf16[640,8,640]{2,0,1:T(8,128)(2,1)} async-done(((bf16[640,8,640]{2,0,1:T(8,128)(2,1)}), bf16[640,8,640]{2,0,1:T(8,128)(2,1)}, u32[]{:S(2)}, u32[]{:S(2)}) %all-to-all-start) | async-done | bytes 6553632 | tf_op jit(solution)/shard_map/all_to_all | solution.py:123
  176.9 9.4 %fusion.1 = bf16[5120,640]{1,0:T(8,128)(2,1)} fusion(bf16[5120,640]{1,0:T(8,128)(2,1)} %param.17, f32[40,640]{1,0:T(8,128)S(1)} %fusion.32, bf16[640,8,640]{2,0,1:T(8,128)(2,1)} %all-to-all-done), kind=kLoop, calls=%fused_computation.2 | loop fusion | flops 16384000 | bytes 19763200 | tf_op jit(solution)/shard_map/convert_element_type | solution.py:135
  186.3 0.0 copy-start.5
  186.3 7.4 %fusion.8 = f32[128,2,5120]{2,0,1:T(8,128)} fusion(bf16[5120,640]{1,0:T(8,128)(2,1)} %fusion.1, bf16[128,2,640]{2,1,0:T(2,128)(2,1)S(1)} %fusion.28), kind=kOutput, calls=%fused_computation.10 | convolution fusion | flops 1677721600 | bytes 12124160 | tf_op jit(solution)/shard_map/dot_general | solution.py:139
  193.7 0.0 copy-start.6
  193.7 0.0 reduce-scatter.2.cloned.1.call-update
  193.7 0.2 all-gather.2.cloned.1.call-start
  194.0 0.0 copy-done.5
  194.0 0.1 iota_compare_fusion.4
  194.1 0.1 add_convert_fusion.2
  194.1 0.3 multiply_cosine_fusion
  194.4 110.2 %reduce-scatter.2.cloned.1.call-done = f32[16,2,5120]{2,0,1:T(8,128)} async-done(((f32[128,2,5120]{2,0,1:T(8,128)}), f32[16,2,5120]{2,0,1:T(8,128)}) %reduce-scatter.2.cloned.1.call-update) | async-done | bytes 655376 | tf_op jit(solution)/shard_map/reduce_scatter | solution.py:138
  304.6 1.2 reshape.160
  305.9 0.1 slice.35
  306.0 0.3 multiply_reduce_fusion
  306.2 0.2 multiply_reduce_fusion.1
  306.4 0.1 copy.81
  306.5 0.1 copy.82
  306.6 0.1 copy.77
  306.8 0.1 copy.78
  306.9 0.0 copy-done.6
  306.9 0.1 multiply_multiply_fusion.1
  307.0 0.0 copy-done.7
  307.0 0.0 slice-start
  307.0 0.2 multiply_multiply_fusion
  307.2 0.1 subtract_convert_fusion.1
  307.4 0.2 subtract_convert_fusion
  307.7 0.0 slice-start.1
  307.7 6.2 %bitcast_reduce_fusion = (f32[16,2,4,8]{3,1,2,0:T(2,128)S(1)}, f32[16,4,2,8,512]{4,3,2,1,0:T(8,128)S(1)}) fusion(pred[16,512]{1,0:T(8,128)(4,1)S(1)} %iota_compare_fusion.4, bf16[16,512,4,128,1]{3,2,1,0,4:T(4,128)(2,1)} %bitcast.81, bf16[16,2,4,8,64]{4,3,1,2,0:T(8,128)(2,1)S(1)} %get-tuple-element.6, bf16[16,2,4,8,64]{4,3,1,2,0:T(8,128)(2,1)S(1)} %get-tuple-element.5), kind=kOutput, calls=%fused_computation.16 | convolution fusion | flops 136313856 | bytes 10760192 | tf_op jit(solution)/shard_map/rsgqd,rlgd->rsgql/dot_general | solution.py:56
  313.9 1.4 fusion.50
  315.3 0.0 slice-done
  315.3 0.0 slice-done.1
  315.3 1.6 fusion.13
  316.9 0.3 fusion.17
  317.3 0.8 convert_element_type.92
  318.1 0.0 all-gather.2.cloned.1.call-update
  318.1 5.4 %copy.126 = bf16[40,2,8,4096]{3,2,0,1:T(8,128)(2,1)} copy(bf16[40,2,8,4096]{3,2,1,0:T(8,128)(2,1)} %bitcast.82) | data formatting | bytes 10485760 | tf_op jit(solution)/shard_map/all_to_all | solution.py:101
  323.6 6.4 %all-to-all-start.1 = ((bf16[320,2,4096]{2,0,1:T(8,128)(2,1)}), bf16[320,2,4096]{2,0,1:T(8,128)(2,1)}, u32[]{:S(2)}, u32[]{:S(2)}) async-start(bf16[320,2,4096]{2,0,1:T(8,128)(2,1)} %bitcast.80), calls=%async_computation.2 | async-start | bytes 10485760 | tf_op jit(solution)/shard_map/all_to_all | solution.py:101
  330.0 0.0 copy-done.3
  330.0 0.4 fusion.30
  330.4 4.6 %all-to-all-done.1 = bf16[320,2,4096]{2,0,1:T(8,128)(2,1)} async-done(((bf16[320,2,4096]{2,0,1:T(8,128)(2,1)}), bf16[320,2,4096]{2,0,1:T(8,128)(2,1)}, u32[]{:S(2)}, u32[]{:S(2)}) %all-to-all-start.1) | async-done | bytes 5242912 | tf_op jit(solution)/shard_map/all_to_all | solution.py:101
  335.0 6.4 %mul.242 = f32[640,32,128]{2,1,0:T(8,128)} broadcast(f32[640,32]{1,0:T(8,128)S(1)} %fusion.30), dimensions={0,1} | broadcast | bytes 10567680 | tf_op jit(solution)/shard_map/mul | solution.py:111
  341.4 17.6 %fusion.3 = bf16[640,4096]{1,0:T(8,128)(2,1)} fusion(f32[80,8,32,128]{3,2,1,0:T(8,128)} %bitcast.78, bf16[640,4096]{1,0:T(8,128)(2,1)} %param.20, bf16[320,2,4096]{2,0,1:T(8,128)(2,1)} %all-to-all-done.1), kind=kLoop, calls=%fused_computation.5 | loop fusion | flops 13107200 | bytes 26214400 | tf_op jit(solution)/shard_map/convert_element_type | solution.py:114
  359.0 8.3 %all-gather.2.cloned.1.call-done = bf16[128,2,4096]{2,0,1:T(8,128)(2,1)} async-done(((bf16[16,2,4096]{2,0,1:T(8,128)(2,1)}), bf16[128,2,4096]{2,0,1:T(8,128)(2,1)}) %all-gather.2.cloned.1.call-update) | async-done | bytes 2097168 | tf_op jit(solution)/shard_map/all_gather | solution.py:148
  367.3 4.9 %fusion.10 = f32[128,2,640]{2,0,1:T(8,128)S(1)} fusion(bf16[128,2,4096]{2,0,1:T(8,128)(2,1)} %all-gather.2.cloned.1.call-done, bf16[640,4096]{1,0:T(8,128)(2,1)} %fusion.3), kind=kOutput, calls=%fused_computation.13 | convolution fusion | flops 1342177280 | bytes 7995392 | tf_op jit(solution)/shard_map/dot_general | solution.py:147
  372.3 5.2 %all-reduce.1 = bf16[128,2,640]{2,0,1:T(8,128)(2,1)S(1)} all-reduce(f32[128,2,640]{2,0,1:T(8,128)S(1)} %fusion.10), channel_id=1, replica_groups=mesh['grp'=2,'fsdp'=8,'tp'=2] {'tp'}, use_global_device_ids=true, to_apply=%region_7.8 | all-reduce | flops 163840 | bytes 983040 | tf_op jit(solution)/shard_map/psum | solution.py:153
  377.5 1.1 copy.88
  378.5 0.0 copy-done.1
  (13 shorter events, 0.2 us)
Async XLA Ops:
  6.5 156.0 %copy-start = (f32[80,40]{0,1:T(8,128)S(1)}, f32[80,40]{0,1:T(8,128)}, u32[]{:S(2)}) copy-start(f32[80,40]{0,1:T(8,128)} %param.19) | copy-start | bytes 38404
  25.5 7.5 %copy-start.2 = (bf16[128,2,640]{2,1,0:T(2,128)(2,1)S(1)}, bf16[128,2,640]{2,1,0:T(2,128)(2,1)}, u32[]{:S(2)}) copy-start(bf16[128,2,640]{2,1,0:T(2,128)(2,1)} %param.13) | copy-start | bytes 983044
  25.5 137.3 %copy-start.4 = (f32[640]{0:T(1024)S(1)}, f32[640]{0:T(1024)}, u32[]{:S(2)}) copy-start(f32[640]{0:T(1024)} %param.14) | copy-start | bytes 7684
  25.5 151.3 %all-to-all-start = ((bf16[640,8,640]{2,0,1:T(8,128)(2,1)}), bf16[640,8,640]{2,0,1:T(8,128)(2,1)}, u32[]{:S(2)}, u32[]{:S(2)}) async-start(bf16[640,8,640]{2,0,1:T(8,128)(2,1)} %copy.74), calls=%async_computation | async-start | bytes 13107200 | tf_op jit(solution)/shard_map/all_to_all | solution.py:123
  32.9 271.7 %reduce-scatter.2.cloned.1.call-start = ((), (), s32[]{:S(2)}) async-start(), calls=%async_computation.3 | async-start | bytes 5898240 | tf_op jit(solution)/shard_map/reduce_scatter | solution.py:138
  186.3 7.7 %copy-start.5 = (s32[16]{0:T(128)S(1)}, s32[16]{0:T(128)}, u32[]{:S(2)}) copy-start(s32[16]{0:T(128)} %param.23) | copy-start | bytes 196
  193.7 113.2 %copy-start.6 = (f32[128]{0:T(128)S(1)}, f32[128]{0:T(128)}, u32[]{:S(2)}) copy-start(f32[128]{0:T(128)} %param.16) | copy-start | bytes 1540
  193.7 113.3 %copy-start.7 = (f32[128]{0:T(128)S(1)}, f32[128]{0:T(128)}, u32[]{:S(2)}) copy-start(f32[128]{0:T(128)} %param.15) | copy-start | bytes 1540
  193.7 173.6 %all-gather.2.cloned.1.call-start = ((), (), s32[]{:S(2)}) async-start(), calls=%async_computation.4 | async-start | bytes 2359296 | tf_op jit(solution)/shard_map/all_gather | solution.py:148
  307.0 8.3 %slice-start = ((s8[8388608]{0:T(1024)(128)(4,1)}), s8[4194304]{0:T(1024)(128)(4,1)S(1)}, s32[]{:S(2)}) async-start(s8[8388608]{0:T(1024)(128)(4,1)} %bitcast.83), calls=%async_computation.5 | async-start | bytes 8388608
  307.7 7.7 %slice-start.1 = ((s8[8388608]{0:T(1024)(128)(4,1)}), s8[4194304]{0:T(1024)(128)(4,1)S(1)}, s32[]{:S(2)}) async-start(s8[8388608]{0:T(1024)(128)(4,1)} %bitcast.83), calls=%async_computation.6 | async-start | bytes 8388608
  323.6 6.4 %copy-start.3 = (f32[40,64]{1,0:T(8,128)S(1)}, f32[40,64]{1,0:T(8,128)}, u32[]{:S(2)}) copy-start(f32[40,64]{1,0:T(8,128)} %param.22) | copy-start | bytes 30724
  323.6 11.4 %all-to-all-start.1 = ((bf16[320,2,4096]{2,0,1:T(8,128)(2,1)}), bf16[320,2,4096]{2,0,1:T(8,128)(2,1)}, u32[]{:S(2)}, u32[]{:S(2)}) async-start(bf16[320,2,4096]{2,0,1:T(8,128)(2,1)} %bitcast.80), calls=%async_computation.2 | async-start | bytes 10485760 | tf_op jit(solution)/shard_map/all_to_all | solution.py:101
  341.4 37.2 %copy-start.1 = (f32[80,40]{0,1:T(8,128)S(1)}, f32[80,40]{0,1:T(8,128)}, u32[]{:S(2)}) copy-start(f32[80,40]{0,1:T(8,128)} %param.19) | copy-start | bytes 38404
Sparse Core Ops, SparseCore 0:
  193.8 110.7 reduce-scatter.1
  318.3 49.0 all-gather.1
where the time goes:
time: 386 us; the launch traced here: 385 us
  waiting for transfers between devices  137 us (35%)
  blocking collectives  134 us (35%)
  local copies, waits for them, and re-layouts  34.6 us (9%)
  other arithmetic  29.6 us (8%)
  matrix products  22.5 us (6%)
  starting transfers between devices  14.1 us (4%)
  between operations  13.7 us (4%)
    psum x1, blocking collectives, on_device(): mean_square = lax.psum(square_part, 'fsdp') / D  129 us
    reduce_scatter x1, waiting for transfers between devices, on_device(): lax.psum_scatter(lax.dot_general(normed, new_qkv, (((2,), (1,)), ((), ())...  110 us
    convert_element_type x1, other arithmetic, on_device(): (base_out.astype(jnp.float32) + delta_out.reshape(out_rows, out_columns))...  17.6 us
    all_to_all x1, waiting for transfers between devices, on_device(): lax.all_to_all(codes_qkv, 'fsdp', split_axis=1, concat_axis=0, tiled=True)  13.6 us
    unnamed x21, local copies, waits for them, and re-layouts  9.55 us
    all_to_all x1, local copies, waits for them, and re-layouts, on_device(): lax.all_to_all(codes_qkv, 'fsdp', split_axis=1, concat_axis=0, tiled=True)  9.45 us
    convert_element_type x1, other arithmetic, on_device(): (base_qkv.astype(jnp.float32) + delta_part.reshape(qkv_rows, width_part))...  9.43 us
    all_gather x1, waiting for transfers between devices, on_device(): lax.all_gather(attended, 'fsdp', axis=0, tiled=True)  8.32 us
  transfers between devices with their start and end apart: 4, of which 4 were waited for; matrix products, arithmetic and copies ran while one was open for 8% of the time, Pallas kernels for 0%

commit v1 on v0

--- a/solution.py
+++ b/solution.py
@@ -1,8 +1,11 @@
+import functools
 import math
 
 import jax
 import jax.numpy as jnp
 from jax import lax
+from jax.experimental import pallas as pl
+from jax.experimental.pallas import tpu as pltpu
 from jax.sharding import PartitionSpec as P
 
 D = 5120
@@ -80,6 +83,232 @@
     return mixed.reshape(row_count, 2, -1).astype(jnp.bfloat16)
 
 
+MESH = pl.DeviceIdType.MESH
+ANY = pl.BlockSpec(memory_space=pl.ANY)
+
+
+def greet(axes):
+    barrier = pltpu.get_barrier_semaphore()
+    total = 0
+    for axis in axes:
+        size = lax.axis_size(axis)
+        me = lax.axis_index(axis)
+        for step in range(1, size):
+            pl.semaphore_signal(
+                barrier, inc=1, device_id={axis: lax.rem(me + step, size)}, device_id_type=MESH
+            )
+        total += size - 1
+    pl.semaphore_wait(barrier, total)
+
+
+def columns_at(index, width):
+    start = index * width
+    return pl.ds(pl.multiple_of(start, 128) if width % 128 == 0 else start, width)
+
+
+def landing(ref, split, rows, index, width):
+    if split:
+        return ref.at[index, rows]
+    return ref.at[rows, columns_at(index, width)]
+
+
+def relay_kernel(split, base, codes, got_base, got_codes, s_base, r_base, s_fwd, r_fwd, s_code, r_code, s_local):
+    groups, shards, halves = lax.axis_size("grp"), lax.axis_size("fsdp"), lax.axis_size("tp")
+    grp, fsdp, tp = lax.axis_index("grp"), lax.axis_index("fsdp"), lax.axis_index("tp")
+    width = base.shape[1]
+    rows = base.shape[0] // shards
+    part = rows // groups
+    code_rows = codes.shape[0]
+    code_width = codes.shape[1] // halves
+    greet(("grp", "fsdp", "tp"))
+    mine = pl.ds(pl.multiple_of(grp * part, 16), part)
+    started = []
+    base_copies = {}
+    for step in range(1, shards):
+        peer = lax.rem(fsdp + step, shards)
+        copy = pltpu.make_async_remote_copy(
+            src_ref=base.at[pl.ds(pl.multiple_of(peer * rows + grp * part, 16), part)],
+            dst_ref=landing(got_base, split, mine, fsdp, width),
+            send_sem=s_base.at[step],
+            recv_sem=r_base.at[step],
+            device_id={"fsdp": peer},
+            device_id_type=MESH,
+        )
+        copy.start()
+        base_copies[step] = copy
+    own_rows = pl.ds(pl.multiple_of(tp * code_rows, 16), code_rows)
+    for step in range(1, halves):
+        peer = lax.rem(tp + step, halves)
+        copy = pltpu.make_async_remote_copy(
+            src_ref=codes.at[:, columns_at(peer, code_width)],
+            dst_ref=got_codes.at[own_rows],
+            send_sem=s_code.at[step],
+            recv_sem=r_code.at[step],
+            device_id={"tp": peer},
+            device_id_type=MESH,
+        )
+        copy.start()
+        started.append(copy)
+    local_codes = pltpu.make_async_copy(
+        codes.at[:, columns_at(tp, code_width)], got_codes.at[own_rows], s_local.at[0]
+    )
+    local_codes.start()
+    local_base = pltpu.make_async_copy(
+        base.at[pl.ds(pl.multiple_of(fsdp * rows, 16), rows)],
+        landing(got_base, split, pl.ds(0, rows), fsdp, width),
+        s_local.at[1],
+    )
+    local_base.start()
+    for step in range(1, shards):
+        base_copies[step].wait_recv()
+        source = lax.rem(fsdp + shards - step, shards)
+        for hop in range(1, groups):
+            block = landing(got_base, split, mine, source, width)
+            copy = pltpu.make_async_remote_copy(
+                src_ref=block,
+                dst_ref=block,
+                send_sem=s_fwd.at[step, hop],
+                recv_sem=r_fwd.at[step, hop],
+                device_id={"grp": lax.rem(grp + hop, groups)},
+                device_id_type=MESH,
+            )
+            copy.start()
+            started.append(copy)
+    for step in range(1, shards):
+        base_copies[step].wait_send()
+    for copy in started:
+        copy.wait()
+    local_codes.wait()
+    local_base.wait()
+
+
+def relay(base, codes, grp_size, shards, halves):
+    width = base.shape[1]
+    rows = base.shape[0] // shards
+    split = width % 128 != 0
+    base_shape = (shards, rows, width) if split else (rows, shards * width)
+    dma = pltpu.SemaphoreType.DMA
+    got_base, got_codes = pl.pallas_call(
+        functools.partial(relay_kernel, split),
+        out_shape=(
+            jax.ShapeDtypeStruct(base_shape, base.dtype),
+            jax.ShapeDtypeStruct((codes.shape[0] * halves, codes.shape[1] // halves), codes.dtype),
+        ),
+        in_specs=[ANY, ANY],
+        out_specs=(ANY, ANY),
+        scratch_shapes=[
+            dma((shards,)), dma((shards,)),
+            dma((shards, grp_size)), dma((shards, grp_size)),
+            dma((halves,)), dma((halves,)), dma((2,)),
+        ],
+        compiler_params=pltpu.CompilerParams(collective_id=0, has_side_effects=True),
+        cost_estimate=pl.CostEstimate(flops=0, bytes_accessed=250_000_000, transcendentals=0),
+        name="relay",
+    )(base, codes)
+    if split:
+        got_base = jnp.swapaxes(got_base, 0, 1).reshape(rows, shards * width)
+    return got_base, got_codes
+
+
+def to_rows_kernel(split, values, got, s_sem, r_sem, s_local):
+    shards = lax.axis_size("fsdp")
+    fsdp = lax.axis_index("fsdp")
+    rows = values.shape[0] // shards
+    width = values.shape[1]
+    greet(("fsdp",))
+    every = pl.ds(0, rows)
+    copies = []
+    for step in range(1, shards):
+        peer = lax.rem(fsdp + step, shards)
+        copy = pltpu.make_async_remote_copy(
+            src_ref=values.at[pl.ds(pl.multiple_of(peer * rows, 8), rows)],
+            dst_ref=landing(got, split, every, fsdp, width),
+            send_sem=s_sem.at[step],
+            recv_sem=r_sem.at[step],
+            device_id={"fsdp": peer},
+            device_id_type=MESH,
+        )
+        copy.start()
+        copies.append(copy)
+    local = pltpu.make_async_copy(
+        values.at[pl.ds(pl.multiple_of(fsdp * rows, 8), rows)],
+        landing(got, split, every, fsdp, width),
+        s_local,
+    )
+    local.start()
+    for copy in copies:
+        copy.wait()
+    local.wait()
+
+
+def to_rows(values, shards):
+    rows = values.shape[0] // shards
+    width = values.shape[1]
+    split = width % 128 != 0
+    dma = pltpu.SemaphoreType.DMA
+    got = pl.pallas_call(
+        functools.partial(to_rows_kernel, split),
+        out_shape=jax.ShapeDtypeStruct(
+            (shards, rows, width) if split else (rows, shards * width), values.dtype
+        ),
+        in_specs=[ANY],
+        out_specs=ANY,
+        scratch_shapes=[dma((shards,)), dma((shards,)), dma],
+        compiler_params=pltpu.CompilerParams(collective_id=1, has_side_effects=True),
+        name="to_rows",
+    )(values)
+    if split:
+        got = jnp.swapaxes(got, 0, 1).reshape(rows, shards * width)
+    return got
+
+
+def updated_matmul_kernel(x, base, codes, scale, out):
+    depth = x.shape[1]
+
+    @pl.when(pl.program_id(0) == 0)
+    def _():
+        out[...] = jnp.zeros_like(out)
+
+    parts = []
+    for block in range(depth // BLOCK):
+        at = slice(block * BLOCK, (block + 1) * BLOCK)
+        delta = codes[:, at].astype(jnp.float32) * scale[0, :, block : block + 1]
+        parts.append((base[:, at].astype(jnp.float32) + delta).astype(jnp.bfloat16))
+    out[...] += lax.dot_general(
+        x[...], jnp.concatenate(parts, axis=1), (((1,), (1,)), ((), ())),
+        preferred_element_type=jnp.float32,
+    )
+
+
+def updated_matmul(x, base, codes, row_scale, depth=512):
+    count, total = base.shape
+    steps = total // depth
+    scale = row_scale.reshape(count, steps, depth // BLOCK).transpose(1, 0, 2)
+    return pl.pallas_call(
+        updated_matmul_kernel,
+        grid=(steps,),
+        out_shape=jax.ShapeDtypeStruct((x.shape[0], count), jnp.float32),
+        in_specs=[
+            pl.BlockSpec((x.shape[0], depth), lambda i: (0, i)),
+            pl.BlockSpec((count, depth), lambda i: (0, i)),
+            pl.BlockSpec((count, depth), lambda i: (0, i)),
+            pl.BlockSpec((1, count, depth // BLOCK), lambda i: (i, 0, 0)),
+        ],
+        out_specs=pl.BlockSpec((x.shape[0], count), lambda i: (0, 0)),
+        compiler_params=pltpu.CompilerParams(vmem_limit_bytes=24 * 2**20),
+        cost_estimate=pl.CostEstimate(
+            flops=2 * x.shape[0] * count * total, bytes_accessed=4 * count * total, transcendentals=0
+        ),
+        name="updated_matmul",
+    )(x, base, codes, scale)
+
+
+def row_scales(scale, first_row, rows):
+    ids = (first_row + jnp.arange(rows, dtype=jnp.int32)) // BLOCK
+    pick = (ids[:, None] == jnp.arange(scale.shape[0], dtype=jnp.int32)[None, :]).astype(jnp.float32)
+    return jnp.dot(pick, scale, precision=lax.Precision.HIGHEST)
+
+
 def on_device(
     hidden,
     input_gain,
@@ -95,62 +324,34 @@
     key_cache,
     value_cache,
 ):
+    grp_size, shards, halves = lax.axis_size("grp"), lax.axis_size("fsdp"), lax.axis_size("tp")
     fsdp_index = lax.axis_index("fsdp")
     tp_index = lax.axis_index("tp")
-    qkv_rows, width_part = base_qkv.shape
-    arrived_out = lax.all_to_all(codes_out, "tp", split_axis=1, concat_axis=0, tiled=True)
+    row_count = hidden.shape[0]
+    whole_hidden = lax.all_gather(hidden.reshape(row_count * 2, -1), "fsdp", axis=1, tiled=True)
+    whole_gain = lax.all_gather(input_gain, "fsdp", axis=0, tiled=True)
+    arrived_base, arrived_out = relay(base_qkv, codes_out, grp_size, shards, halves)
+
+    hidden_float = whole_hidden.astype(jnp.float32)
+    mean_square = jnp.sum(hidden_float * hidden_float, axis=-1) / D
+    normed = (hidden_float * lax.rsqrt(mean_square + epsilon)[..., None] * whole_gain).astype(
+        jnp.bfloat16
+    )
+    qkv_rows = codes_qkv.shape[0]
+    qkv_scale = row_scales(scale_qkv, (tp_index * shards + fsdp_index) * qkv_rows, qkv_rows)
+    projected = updated_matmul(normed, arrived_base, codes_qkv, qkv_scale)
+    projected = to_rows(projected, shards).reshape(row_count // shards, 2, -1)
+    attended = attend(projected, lengths, key_cache, value_cache, q_gain, k_gain)
+
     out_rows, out_columns = base_out.shape
     column_blocks = out_columns // BLOCK
     scale_columns = lax.dynamic_slice_in_dim(scale_out, tp_index * column_blocks, column_blocks, 1)
-    row_ids = (fsdp_index * out_rows + jnp.arange(out_rows, dtype=jnp.int32)) // BLOCK
-    row_pick = (
-        row_ids[:, None] == jnp.arange(scale_out.shape[0], dtype=jnp.int32)[None, :]
-    ).astype(jnp.float32)
-    row_scale = jnp.dot(row_pick, scale_columns, precision=lax.Precision.HIGHEST)
-    delta_out = (
-        arrived_out.astype(jnp.float32).reshape(out_rows, column_blocks, BLOCK)
-        * row_scale[:, :, None]
-    )
-    new_out = (base_out.astype(jnp.float32) + delta_out.reshape(out_rows, out_columns)).astype(
-        jnp.bfloat16
-    )
-    hidden_float = hidden.astype(jnp.float32)
-    square_part = jnp.sum(hidden_float * hidden_float, axis=-1)
-    mean_square = lax.psum(square_part, "fsdp") / D
-    normed = (hidden_float * lax.rsqrt(mean_square + epsilon)[..., None] * input_gain).astype(
-        jnp.bfloat16
-    )
-    arrived = lax.all_to_all(codes_qkv, "fsdp", split_axis=1, concat_axis=0, tiled=True)
-    row_blocks = qkv_rows // BLOCK
-    scale_rows = lax.dynamic_slice_in_dim(scale_qkv, tp_index * row_blocks, row_blocks, 0)
-    column_ids = (fsdp_index * width_part + jnp.arange(width_part, dtype=jnp.int32)) // BLOCK
-    column_pick = (
-        jnp.arange(scale_qkv.shape[1], dtype=jnp.int32)[:, None] == column_ids[None, :]
-    ).astype(jnp.float32)
-    column_scale = jnp.dot(scale_rows, column_pick, precision=lax.Precision.HIGHEST)
-    delta_part = (
-        arrived.astype(jnp.float32).reshape(row_blocks, BLOCK, width_part)
-        * column_scale[:, None, :]
-    )
-    new_qkv = (base_qkv.astype(jnp.float32) + delta_part.reshape(qkv_rows, width_part)).astype(
-        jnp.bfloat16
-    )
-    projected = lax.psum_scatter(
-        lax.dot_general(
-            normed, new_qkv, (((2,), (1,)), ((), ())), preferred_element_type=jnp.float32
-        ),
-        "fsdp",
-        scatter_dimension=0,
-        tiled=True,
-    )
-    attended = attend(projected, lengths, key_cache, value_cache, q_gain, k_gain)
-    partial_out = lax.dot_general(
-        lax.all_gather(attended, "fsdp", axis=0, tiled=True),
-        new_out,
-        (((2,), (1,)), ((), ())),
-        preferred_element_type=jnp.float32,
-    )
-    return lax.psum(partial_out, "tp").astype(jnp.bfloat16)
+    out_scale = row_scales(scale_columns, fsdp_index * out_rows, out_rows)
+    whole_attended = lax.all_gather(
+        attended.reshape(-1, attended.shape[-1]), "fsdp", axis=0, tiled=True
+    )
+    partial_out = updated_matmul(whole_attended, base_out, arrived_out, out_scale)
+    return lax.psum(partial_out, "tp").astype(jnp.bfloat16).reshape(row_count, 2, out_rows)
 
 
 def solution(mesh):

time: 386 us -> 306 us (0.79)
  Pallas kernels: 0 us -> 139 us
  waiting for transfers between devices: 137 us -> 49.8 us
  blocking collectives: 134 us -> 67.7 us
  other arithmetic: 29.6 us -> 6.86 us
  local copies, waits for them, and re-layouts: 34.6 us -> 17.5 us
  starting transfers between devices: 14.1 us -> 0.04 us
  matrix products: 22.5 us -> 10.3 us
    pallas_call x0 -> x4, Pallas kernels: none -> 139 us  [the longest x1 112 us: relay(): pl.pallas_call(functools.partial(relay_kernel, split), out_shape=(jax.Sha...]
    psum x2 -> x1, blocking collectives: 134 us -> 5.17 us  [on_device(): lax.psum(partial_out, 'tp').astype(jnp.bfloat16)]
    reduce_scatter x1 -> x0, waiting for transfers between devices: 110 us -> none  [on_device(): lax.psum_scatter(lax.dot_general(normed, new_qkv, (((2,), (1,)), ((), ())...]
    all_gather x0 -> x1, blocking collectives: none -> 62.6 us  [on_device(): whole_gain = lax.all_gather(input_gain, 'fsdp', axis=0, tiled=True)]
    all_gather x1 -> x2, waiting for transfers between devices: 8.32 us -> 49.8 us  [the longest x1 49.8 us: on_device(): lax.all_gather(attended.reshape(-1, attended.shape[-1]), 'fsdp', axis=0,...]
    convert_element_type x3 -> x1, other arithmetic: 27.5 us -> 2.66 us  [on_device(): (hidden_float * lax.rsqrt(mean_square + epsilon)[..., None] * whole_gain)...]
    all_to_all x2 -> x0, waiting for transfers between devices: 18.2 us -> none  [the longest x1 13.6 us: on_device(): lax.all_to_all(codes_qkv, 'fsdp', split_axis=1, concat_axis=0, tiled=True)]
    all_to_all x2 -> x0, local copies, waits for them, and re-layouts: 14.9 us -> none  [the longest x1 9.45 us: on_device(): lax.all_to_all(codes_qkv, 'fsdp', split_axis=1, concat_axis=0, tiled=True)]
  transfers between devices with their start and end apart: 4 -> 2, of which waited for: 4 -> 1; matrix products, arithmetic and copies ran while one was open for 8% -> 1% of each run, Pallas kernels for 0% -> 37%
where the time goes in v1:
time: 306 us; the launch traced here: 305 us
  Pallas kernels  139 us (45%)
  blocking collectives  67.7 us (22%)
  waiting for transfers between devices  49.8 us (16%)
  local copies, waits for them, and re-layouts  17.5 us (6%)
  between operations  13.8 us (5%)
  matrix products  10.3 us (3%)
  other arithmetic  6.86 us (2%)
    pallas_call x1, Pallas kernels, relay(): pl.pallas_call(functools.partial(relay_kernel, split), out_shape=(jax.Sha...  112 us
    all_gather x1, blocking collectives, on_device(): whole_gain = lax.all_gather(input_gain, 'fsdp', axis=0, tiled=True)  62.6 us
    all_gather x1, waiting for transfers between devices, on_device(): lax.all_gather(attended.reshape(-1, attended.shape[-1]), 'fsdp', axis=0,...  49.8 us
    pallas_call x2, Pallas kernels, updated_matmul(): pl.pallas_call(updated_matmul_kernel, grid=(steps,), out_shape=jax.ShapeD...  15.7 us
    pallas_call x1, Pallas kernels, to_rows(): pl.pallas_call(functools.partial(to_rows_kernel, split), out_shape=jax.Sh...  11.6 us
    unnamed x31, local copies, waits for them, and re-layouts  10.3 us
    dot_general x1, matrix products, attend(): jnp.einsum('rsgqd,rlgd->rsgql', queries, key_cache, preferred_element_typ...  6.19 us
  transfers between devices with their start and end apart: 2, of which 1 were waited for; matrix products, arithmetic and copies ran while one was open for 1% of the time, Pallas kernels for 37%

profile of v1, /device:TPU:0, one launch (start us, length us, event | category | flops | bytes accessed | tf_op | source)
XLA Modules:
  0.0 305.3 jit_solution(14335161572872058489)
XLA Ops:
  6.5 0.0 copy-start
  6.5 0.0 copy-start.9
  6.5 0.0 all-gather.4.cloned.1.call-start
  6.5 1.8 reshape.153
  8.4 0.0 all-gather.4.cloned.1.call-update
  8.4 0.0 all-gather.6.cloned.1.call-start
  8.5 0.0 copy-done
  8.5 0.4 fusion.21
  9.0 1.1 copy.46
  10.1 0.0 copy-done.9
  10.1 0.0 copy-start.10
  10.1 111.9 %relay.1 = (bf16[640,5120]{1,0:T(8,128)(2,1)}, bf16[640,4096]{1,0:T(8,128)(2,1)}) custom-call(bf16[5120,640]{1,0:T(8,128)(2,1)} %base.2, bf16[320,8192]{1,0:T(8,128)(2,1)} %codes.2), custom_call_target="tpu_custom_call" | custom-call | bytes 250000000 | tf_op jit(solution)/shard_map/relay/pallas_call | solution.py:191
  122.0 62.6 %all-gather = f32[8,1,640]{2,1,0:T(1,128)S(1)} all-gather(f32[1,1,640]{2,1,0:T(1,128)S(1)} %reshape.157), channel_id=1, replica_groups=mesh['grp'=2,'fsdp'=8,'tp'=2] {'fsdp'}, dimensions={0}, use_global_device_ids=true | all-gather | bytes 23040 | tf_op jit(solution)/shard_map/all_gather | solution.py:332
  184.6 0.0 copy-done.10
  184.6 0.1 add_convert_fusion.2
  184.6 0.1 iota_compare_fusion.4
  184.7 0.3 multiply_cosine_fusion
  185.0 0.0 all-gather.4.cloned.1.call-done
  185.1 0.0 copy-start.3
  185.1 2.5 fusion.4
  187.6 2.7 fusion.6.x
  190.2 0.0 copy-done.3
  190.2 0.0 copy-start.2
  190.3 2.9 copy-done.2
  193.1 8.7 %updated_matmul.2.values = f32[256,640]{1,0:T(8,128)S(1)} custom-call(bf16[256,5120]{1,0:T(8,128)(2,1)S(1)} %fusion.6.x, bf16[640,5120]{1,0:T(8,128)(2,1)S(1)} %copy-done.3, bf16[640,5120]{1,0:T(8,128)(2,1)S(1)} %copy-done.2, f32[10,640,4]{2,1,0:T(8,128)S(1)} %bitcast.49), custom_call_target="tpu_custom_call" | custom-call | flops 1677721600 | bytes 13107200 | tf_op jit(solution)/shard_map/updated_matmul/pallas_call | solution.py:287
  201.8 0.0 copy-start.6
  201.8 0.8 copy-done.6
  202.6 11.6 %to_rows.1 = f32[32,5120]{1,0:T(8,128)} custom-call(f32[256,640]{1,0:T(8,128)} %copy-done.6), custom_call_target="tpu_custom_call" | custom-call | tf_op jit(solution)/shard_map/to_rows/pallas_call | solution.py:249
  214.3 1.2 reshape_reshape.3
  215.5 0.3 multiply_reduce_fusion
  215.8 0.1 slice.35
  215.9 0.2 multiply_reduce_fusion.1
  216.1 0.1 copy.52
  216.2 0.1 copy.53
  216.3 0.1 copy.48
  216.4 0.1 copy.49
  216.5 0.0 copy-done.11
  216.5 0.1 multiply_multiply_fusion.1
  216.7 0.0 copy-done.12
  216.7 0.0 slice-start
  216.7 0.2 multiply_multiply_fusion
  216.9 0.1 subtract_convert_fusion.1
  217.0 0.2 subtract_convert_fusion
  217.3 0.0 slice-start.1
  217.3 6.2 %bitcast_reduce_fusion = (f32[16,2,4,8]{3,1,2,0:T(2,128)S(1)}, f32[16,4,2,8,512]{4,3,2,1,0:T(8,128)S(1)}) fusion(pred[16,512]{1,0:T(8,128)(4,1)S(1)} %iota_compare_fusion.4, bf16[16,512,4,128,1]{3,2,1,0,4:T(4,128)(2,1)} %bitcast.51, bf16[16,2,4,8,64]{4,3,1,2,0:T(8,128)(2,1)S(1)} %get-tuple-element.10, bf16[16,2,4,8,64]{4,3,1,2,0:T(8,128)(2,1)S(1)} %get-tuple-element.9), kind=kOutput, calls=%fused_computation.10 | convolution fusion | flops 136313856 | bytes 10760192 | tf_op jit(solution)/shard_map/rsgqd,rlgd->rsgql/dot_general | solution.py:59
  223.5 1.4 fusion.42
  225.0 0.0 slice-done
  225.0 0.0 slice-done.1
  225.0 1.6 fusion.8
  226.6 0.0 copy-start.8
  226.6 0.3 fusion.12
  226.9 0.8 convert_element_type.54
  227.8 0.0 all-gather.6.cloned.1.call-update
  227.8 0.0 copy-done.8
  227.8 0.4 fusion.22
  228.3 0.8 copy.57
  229.1 49.8 %all-gather.6.cloned.1.call-done.x = bf16[256,4096]{1,0:T(8,128)(2,1)} async-done(((bf16[32,4096]{1,0:T(8,128)(2,1)}), bf16[256,4096]{1,0:T(8,128)(2,1)}) %all-gather.6.cloned.1.call-update) | async-done | bytes 2097168 | tf_op jit(solution)/shard_map/all_gather | solution.py:350
  278.8 2.5 copy-done.4
  281.3 2.5 copy-done.5
  283.8 1.6 copy-done.7
  285.4 7.0 %updated_matmul.3 = f32[256,640]{1,0:T(8,128)S(1)} custom-call(bf16[256,4096]{1,0:T(8,128)(2,1)S(1)} %copy-done.7, bf16[640,4096]{1,0:T(8,128)(2,1)S(1)} %copy-done.4, bf16[640,4096]{1,0:T(8,128)(2,1)S(1)} %copy-done.5, f32[8,640,4]{2,1,0:T(8,128)S(1)} %bitcast.50), custom_call_target="tpu_custom_call" | custom-call | flops 1342177280 | bytes 10485760 | tf_op jit(solution)/shard_map/updated_matmul/pallas_call | solution.py:287
  292.4 5.2 %all-reduce.1 = bf16[256,640]{1,0:T(8,128)(2,1)S(1)} all-reduce(f32[256,640]{1,0:T(8,128)S(1)} %updated_matmul.3), channel_id=1, replica_groups=mesh['grp'=2,'fsdp'=8,'tp'=2] {'tp'}, use_global_device_ids=true, to_apply=%region_5.6 | all-reduce | flops 163840 | bytes 983040 | tf_op jit(solution)/shard_map/psum | solution.py:354
  297.6 0.8 reshape.156
  298.5 0.0 copy-done.1
  (20 shorter events, 0.3 us)
Async XLA Ops:
  6.5 2.0 copy-start
  6.5 3.5 %copy-start.9 = (f32[640]{0:T(1024)S(1)}, f32[640]{0:T(1024)}, u32[]{:S(2)}) copy-start(f32[640]{0:T(1024)} %param.14) | copy-start | bytes 7684
  6.5 178.5 %all-gather.4.cloned.1.call-start = ((), (), s32[]{:S(2)}) async-start(), calls=%async_computation | async-start | bytes 2949120 | tf_op jit(solution)/shard_map/all_gather | solution.py:331
  8.4 270.4 %all-gather.6.cloned.1.call-start = ((), (), s32[]{:S(2)}) async-start(), calls=%async_computation.1 | async-start | bytes 2359296 | tf_op jit(solution)/shard_map/all_gather | solution.py:350
  10.1 174.5 %copy-start.10 = (s32[16]{0:T(128)S(1)}, s32[16]{0:T(128)}, u32[]{:S(2)}) copy-start(s32[16]{0:T(128)} %param.23) | copy-start | bytes 196
  185.1 5.2 %copy-start.3 = (bf16[640,5120]{1,0:T(8,128)(2,1)S(1)}, bf16[640,5120]{1,0:T(8,128)(2,1)}, u32[]{:S(2)}) copy-start(bf16[640,5120]{1,0:T(8,128)(2,1)} %get-tuple-element.7.base) | copy-start | bytes 19660804
  190.2 2.9 copy-start.2
  201.8 0.8 copy-start.6
  202.6 13.9 %copy-start.11 = (f32[128]{0:T(128)S(1)}, f32[128]{0:T(128)}, u32[]{:S(2)}) copy-start(f32[128]{0:T(128)} %param.16) | copy-start | bytes 1540
  202.6 14.1 %copy-start.12 = (f32[128]{0:T(128)S(1)}, f32[128]{0:T(128)}, u32[]{:S(2)}) copy-start(f32[128]{0:T(128)} %param.15) | copy-start | bytes 1540
  216.7 8.3 %slice-start = ((s8[8388608]{0:T(1024)(128)(4,1)}), s8[4194304]{0:T(1024)(128)(4,1)S(1)}, s32[]{:S(2)}) async-start(s8[8388608]{0:T(1024)(128)(4,1)} %bitcast.53), calls=%async_computation.2 | async-start | bytes 8388608
  217.3 7.7 %slice-start.1 = ((s8[8388608]{0:T(1024)(128)(4,1)}), s8[4194304]{0:T(1024)(128)(4,1)S(1)}, s32[]{:S(2)}) async-start(s8[8388608]{0:T(1024)(128)(4,1)} %bitcast.53), calls=%async_computation.3 | async-start | bytes 8388608
  226.6 1.2 copy-start.8
  278.8 2.5 copy-start.4
  281.3 2.5 copy-start.5
  283.8 1.6 copy-start.7
  285.4 13.1 %copy-start.1 = (f32[80,40]{0,1:T(8,128)S(1)}, f32[80,40]{0,1:T(8,128)}, u32[]{:S(2)}) copy-start(f32[80,40]{0,1:T(8,128)} %param.19) | copy-start | bytes 38404
Sparse Core Ops, SparseCore 0:
  9.6 97.0 all-gather.3
  227.9 50.8 all-gather.5

commit v2 on v1

--- a/solution.py
+++ b/solution.py
@@ -112,102 +112,249 @@
     return ref.at[rows, columns_at(index, width)]
 
 
-def relay_kernel(split, base, codes, got_base, got_codes, s_base, r_base, s_fwd, r_fwd, s_code, r_code, s_local):
+def folds(shards):
+    inner = 2 if shards % 2 == 0 else 1
+    return shards // inner, inner
+
+
+def send(source, target, s_sem, r_sem, device):
+    copy = pltpu.make_async_remote_copy(
+        src_ref=source, dst_ref=target, send_sem=s_sem, recv_sem=r_sem,
+        device_id=device, device_id_type=MESH,
+    )
+    copy.start()
+    return copy
+
+
+class Spread:
+    def __init__(self, own, place, sems, over_tp):
+        self.own, self.place, self.over_tp = own, place, over_tp
+        self.s_sem, self.r_sem, self.s_tp, self.r_tp = sems
+        self.shards = lax.axis_size("fsdp")
+        self.outer, self.inner = folds(self.shards)
+        fsdp = lax.axis_index("fsdp")
+        self.hi, self.lo = fsdp // self.inner, lax.rem(fsdp, self.inner)
+        self.arriving = {}
+        self.sent = []
+
+    def begin(self):
+        fsdp = lax.axis_index("fsdp")
+        for a in range(1, self.outer):
+            at = a * self.inner
+            peer = lax.rem(self.hi + a, self.outer) * self.inner + self.lo
+            self.arriving[a, 0] = send(
+                self.own, self.place(fsdp), self.s_sem.at[at], self.r_sem.at[at], {"fsdp": peer}
+            )
+        self.inward(0, self.own)
+
+    def inward(self, a, block):
+        source_hi = lax.rem(self.hi + self.outer - a, self.outer)
+        for b in range(1, self.inner):
+            at = a * self.inner + b
+            peer = self.hi * self.inner + lax.rem(self.lo + b, self.inner)
+            self.arriving[a, b] = send(
+                block, self.place(source_hi * self.inner + self.lo),
+                self.s_sem.at[at], self.r_sem.at[at], {"fsdp": peer},
+            )
+
+    def across(self, a, b):
+        if not self.over_tp:
+            return
+        halves = lax.axis_size("tp")
+        tp = lax.axis_index("tp")
+        source = lax.rem(self.hi + self.outer - a, self.outer) * self.inner + lax.rem(
+            self.lo + self.inner - b, self.inner
+        )
+        block = self.place(source)
+        for c in range(1, halves):
+            at = (a * self.inner + b, c)
+            self.sent.append(
+                send(block, block, self.s_tp.at[at], self.r_tp.at[at], {"tp": lax.rem(tp + c, halves)})
+            )
+
+    def pass_on(self):
+        for a in range(1, self.outer):
+            self.arriving[a, 0].wait_recv()
+            source = lax.rem(self.hi + self.outer - a, self.outer) * self.inner + self.lo
+            self.inward(a, self.place(source))
+            self.across(a, 0)
+        for a in range(self.outer):
+            for b in range(1, self.inner):
+                self.arriving[a, b].wait_recv()
+                self.across(a, b)
+
+    def end(self):
+        for copy in self.arriving.values():
+            copy.wait_send()
+        for copy in self.sent:
+            copy.wait()
+
+
+def chunks_of(rows):
+    return 2 if rows % 32 == 0 else 1
+
+
+def relay_kernel(
+    split, base, codes, hidden, gain, got_base, got_codes, got_hidden, got_gain,
+    s_base, r_base, s_fwd, r_fwd, s_code, r_code, s_hid, r_hid, s_htp, r_htp, s_gain, r_gain, s_local,
+):
     groups, shards, halves = lax.axis_size("grp"), lax.axis_size("fsdp"), lax.axis_size("tp")
     grp, fsdp, tp = lax.axis_index("grp"), lax.axis_index("fsdp"), lax.axis_index("tp")
     width = base.shape[1]
     rows = base.shape[0] // shards
     part = rows // groups
+    chunks = chunks_of(part)
+    size = part // chunks
     code_rows = codes.shape[0]
     code_width = codes.shape[1] // halves
+    hidden_part = hidden.shape[0] // halves
+    outer, inner = folds(shards)
     greet(("grp", "fsdp", "tp"))
-    mine = pl.ds(pl.multiple_of(grp * part, 16), part)
+
+    hidden_rows = pl.ds(pl.multiple_of(tp * hidden_part, 16), hidden_part)
+    spread = Spread(
+        hidden.at[hidden_rows],
+        lambda source: landing(got_hidden, split, hidden_rows, source, width),
+        (s_hid, r_hid, s_htp, r_htp),
+        True,
+    )
+    spread.begin()
+
+    def my_rows(chunk, first):
+        return pl.ds(pl.multiple_of(first + grp * part + chunk * size, 16), size)
+
     started = []
-    base_copies = {}
-    for step in range(1, shards):
-        peer = lax.rem(fsdp + step, shards)
-        copy = pltpu.make_async_remote_copy(
-            src_ref=base.at[pl.ds(pl.multiple_of(peer * rows + grp * part, 16), part)],
-            dst_ref=landing(got_base, split, mine, fsdp, width),
-            send_sem=s_base.at[step],
-            recv_sem=r_base.at[step],
-            device_id={"fsdp": peer},
-            device_id_type=MESH,
-        )
-        copy.start()
-        base_copies[step] = copy
+    base_copies = []
+    hi, lo = fsdp // inner, lax.rem(fsdp, inner)
+    for a in range(outer):
+        for b in range(inner):
+            if a == 0 and b == 0:
+                continue
+            peer = lax.rem(hi + a, outer) * inner + lax.rem(lo + b, inner)
+            source = lax.rem(hi + outer - a, outer) * inner + lax.rem(lo + inner - b, inner)
+            step = a * inner + b
+            started.append(
+                send(
+                    gain, got_gain.at[fsdp], s_gain.at[step], r_gain.at[step], {"fsdp": peer}
+                )
+            )
+            for chunk in range(chunks):
+                at = (step, chunk)
+                copy = send(
+                    base.at[my_rows(chunk, peer * rows)],
+                    landing(got_base, split, my_rows(chunk, 0), fsdp, width),
+                    s_base.at[at], r_base.at[at], {"fsdp": peer},
+                )
+                base_copies.append((copy, step, chunk, source))
     own_rows = pl.ds(pl.multiple_of(tp * code_rows, 16), code_rows)
     for step in range(1, halves):
         peer = lax.rem(tp + step, halves)
-        copy = pltpu.make_async_remote_copy(
-            src_ref=codes.at[:, columns_at(peer, code_width)],
-            dst_ref=got_codes.at[own_rows],
-            send_sem=s_code.at[step],
-            recv_sem=r_code.at[step],
-            device_id={"tp": peer},
-            device_id_type=MESH,
+        started.append(
+            send(
+                codes.at[:, columns_at(peer, code_width)], got_codes.at[own_rows],
+                s_code.at[step], r_code.at[step], {"tp": peer},
+            )
         )
+    local = [
+        pltpu.make_async_copy(
+            codes.at[:, columns_at(tp, code_width)], got_codes.at[own_rows], s_local.at[0]
+        ),
+        pltpu.make_async_copy(
+            base.at[pl.ds(pl.multiple_of(fsdp * rows, 16), rows)],
+            landing(got_base, split, pl.ds(0, rows), fsdp, width),
+            s_local.at[1],
+        ),
+        pltpu.make_async_copy(
+            hidden, landing(got_hidden, split, pl.ds(0, hidden.shape[0]), fsdp, width), s_local.at[2]
+        ),
+        pltpu.make_async_copy(gain, got_gain.at[fsdp], s_local.at[3]),
+    ]
+    for copy in local:
         copy.start()
-        started.append(copy)
-    local_codes = pltpu.make_async_copy(
-        codes.at[:, columns_at(tp, code_width)], got_codes.at[own_rows], s_local.at[0]
-    )
-    local_codes.start()
-    local_base = pltpu.make_async_copy(
-        base.at[pl.ds(pl.multiple_of(fsdp * rows, 16), rows)],
-        landing(got_base, split, pl.ds(0, rows), fsdp, width),
-        s_local.at[1],
-    )
-    local_base.start()
-    for step in range(1, shards):
-        base_copies[step].wait_recv()
-        source = lax.rem(fsdp + shards - step, shards)
+    spread.pass_on()
+    for copy, step, chunk, source in base_copies:
+        copy.wait_recv()
+        block = landing(got_base, split, my_rows(chunk, 0), source, width)
         for hop in range(1, groups):
-            block = landing(got_base, split, mine, source, width)
-            copy = pltpu.make_async_remote_copy(
-                src_ref=block,
-                dst_ref=block,
-                send_sem=s_fwd.at[step, hop],
-                recv_sem=r_fwd.at[step, hop],
-                device_id={"grp": lax.rem(grp + hop, groups)},
-                device_id_type=MESH,
-            )
-            copy.start()
-            started.append(copy)
-    for step in range(1, shards):
-        base_copies[step].wait_send()
+            at = (step * chunks + chunk, hop)
+            started.append(
+                send(
+                    block, block, s_fwd.at[at], r_fwd.at[at], {"grp": lax.rem(grp + hop, groups)}
+                )
+            )
+    spread.end()
+    for copy, _, _, _ in base_copies:
+        copy.wait_send()
     for copy in started:
         copy.wait()
-    local_codes.wait()
-    local_base.wait()
-
-
-def relay(base, codes, grp_size, shards, halves):
+    for copy in local:
+        copy.wait()
+
+
+def relay(base, codes, hidden, gain, grp_size, shards, halves):
     width = base.shape[1]
     rows = base.shape[0] // shards
+    chunks = chunks_of(rows // grp_size)
     split = width % 128 != 0
-    base_shape = (shards, rows, width) if split else (rows, shards * width)
+
+    def gathered(count):
+        return (shards, count, width) if split else (count, shards * width)
+
     dma = pltpu.SemaphoreType.DMA
-    got_base, got_codes = pl.pallas_call(
+    got_base, got_codes, got_hidden, got_gain = pl.pallas_call(
         functools.partial(relay_kernel, split),
         out_shape=(
-            jax.ShapeDtypeStruct(base_shape, base.dtype),
+            jax.ShapeDtypeStruct(gathered(rows), base.dtype),
             jax.ShapeDtypeStruct((codes.shape[0] * halves, codes.shape[1] // halves), codes.dtype),
-        ),
-        in_specs=[ANY, ANY],
-        out_specs=(ANY, ANY),
+            jax.ShapeDtypeStruct(gathered(hidden.shape[0]), hidden.dtype),
+            jax.ShapeDtypeStruct((shards, 8, width), gain.dtype),
+        ),
+        in_specs=[ANY] * 4,
+        out_specs=(ANY,) * 4,
         scratch_shapes=[
-            dma((shards,)), dma((shards,)),
-            dma((shards, grp_size)), dma((shards, grp_size)),
-            dma((halves,)), dma((halves,)), dma((2,)),
+            dma((shards, chunks)), dma((shards, chunks)),
+            dma((shards * chunks, grp_size)), dma((shards * chunks, grp_size)),
+            dma((halves,)), dma((halves,)),
+            dma((shards,)), dma((shards,)), dma((shards, halves)), dma((shards, halves)),
+            dma((shards,)), dma((shards,)), dma((4,)),
         ],
         compiler_params=pltpu.CompilerParams(collective_id=0, has_side_effects=True),
         cost_estimate=pl.CostEstimate(flops=0, bytes_accessed=250_000_000, transcendentals=0),
         name="relay",
-    )(base, codes)
+    )(base, codes, hidden, jnp.broadcast_to(gain[None], (8, width)))
     if split:
         got_base = jnp.swapaxes(got_base, 0, 1).reshape(rows, shards * width)
-    return got_base, got_codes
+        got_hidden = jnp.swapaxes(got_hidden, 0, 1).reshape(-1, shards * width)
+    return got_base, got_codes, got_hidden, got_gain[:, 0].reshape(-1)
+
+
+def gather_kernel(values, got, s_sem, r_sem, s_local):
+    rows = values.shape[0]
+    greet(("fsdp",))
+
+    def place(source):
+        return got.at[pl.ds(pl.multiple_of(source * rows, 16), rows)]
+
+    spread = Spread(values, place, (s_sem, r_sem, None, None), False)
+    spread.begin()
+    local = pltpu.make_async_copy(values, place(lax.axis_index("fsdp")), s_local)
+    local.start()
+    spread.pass_on()
+    spread.end()
+    local.wait()
+
+
+def gather_rows(values, shards):
+    dma = pltpu.SemaphoreType.DMA
+    return pl.pallas_call(
+        gather_kernel,
+        out_shape=jax.ShapeDtypeStruct((values.shape[0] * shards, values.shape[1]), values.dtype),
+        in_specs=[ANY],
+        out_specs=ANY,
+        scratch_shapes=[dma((shards,)), dma((shards,)), dma],
+        compiler_params=pltpu.CompilerParams(collective_id=2, has_side_effects=True),
+        name="gather_rows",
+    )(values)
 
 
 def to_rows_kernel(split, values, got, s_sem, r_sem, s_local):
@@ -295,7 +442,7 @@
             pl.BlockSpec((1, count, depth // BLOCK), lambda i: (i, 0, 0)),
         ],
         out_specs=pl.BlockSpec((x.shape[0], count), lambda i: (0, 0)),
-        compiler_params=pltpu.CompilerParams(vmem_limit_bytes=24 * 2**20),
+        compiler_params=pltpu.CompilerParams(vmem_limit_bytes=56 * 2**20),
         cost_estimate=pl.CostEstimate(
             flops=2 * x.shape[0] * count * total, bytes_accessed=4 * count * total, transcendentals=0
         ),
@@ -328,9 +475,9 @@
     fsdp_index = lax.axis_index("fsdp")
     tp_index = lax.axis_index("tp")
     row_count = hidden.shape[0]
-    whole_hidden = lax.all_gather(hidden.reshape(row_count * 2, -1), "fsdp", axis=1, tiled=True)
-    whole_gain = lax.all_gather(input_gain, "fsdp", axis=0, tiled=True)
-    arrived_base, arrived_out = relay(base_qkv, codes_out, grp_size, shards, halves)
+    arrived_base, arrived_out, whole_hidden, whole_gain = relay(
+        base_qkv, codes_out, hidden.reshape(row_count * 2, -1), input_gain, grp_size, shards, halves
+    )
 
     hidden_float = whole_hidden.astype(jnp.float32)
     mean_square = jnp.sum(hidden_float * hidden_float, axis=-1) / D
@@ -347,9 +494,7 @@
     column_blocks = out_columns // BLOCK
     scale_columns = lax.dynamic_slice_in_dim(scale_out, tp_index * column_blocks, column_blocks, 1)
     out_scale = row_scales(scale_columns, fsdp_index * out_rows, out_rows)
-    whole_attended = lax.all_gather(
-        attended.reshape(-1, attended.shape[-1]), "fsdp", axis=0, tiled=True
-    )
+    whole_attended = gather_rows(attended.reshape(-1, attended.shape[-1]), shards)
     partial_out = updated_matmul(whole_attended, base_out, arrived_out, out_scale)
     return lax.psum(partial_out, "tp").astype(jnp.bfloat16).reshape(row_count, 2, out_rows)
 

time: 306 us -> 237 us (0.77)
  Pallas kernels: 139 us -> 201 us
  blocking collectives: 67.7 us -> 5.94 us
  waiting for transfers between devices: 49.8 us -> 0 us
  between operations: 13.8 us -> 0.31 us
  local copies, waits for them, and re-layouts: 17.5 us -> 12.4 us
    all_gather x1 -> x0, blocking collectives: 62.6 us -> none  [on_device(): whole_gain = lax.all_gather(input_gain, 'fsdp', axis=0, tiled=True)]
    all_gather x2 -> x0, waiting for transfers between devices: 49.8 us -> none  [the longest x1 49.8 us: on_device(): lax.all_gather(attended.reshape(-1, attended.shape[-1]), 'fsdp', axis=0,...]
    pallas_call x0 -> x1, Pallas kernels: none -> 35.8 us  [gather_rows(): pl.pallas_call(gather_kernel, out_shape=jax.ShapeDtypeStruct((values.shap...]
    pallas_call x1, Pallas kernels: 112 us -> 123 us  [relay(): pl.pallas_call(functools.partial(relay_kernel, split), out_shape=(jax.Sha...]
    unnamed x31 -> x18, local copies, waits for them, and re-layouts: 10.3 us -> 0.04 us
    pallas_call x2, Pallas kernels: 15.7 us -> 24 us  [updated_matmul(): pl.pallas_call(updated_matmul_kernel, grid=(steps,), out_shape=jax.ShapeD...]
    pallas_call x1, Pallas kernels: 11.6 us -> 17.8 us  [to_rows(): pl.pallas_call(functools.partial(to_rows_kernel, split), out_shape=jax.Sh...]
  transfers between devices with their start and end apart: 2 -> 0, of which waited for: 1 -> 0; matrix products, arithmetic and copies ran while one was open for 1% -> 0% of each run, Pallas kernels for 37% -> 0%
where the time goes in v2:
time: 237 us; the launch traced here: 236 us
  Pallas kernels  201 us (85%)
  local copies, waits for them, and re-layouts  12.4 us (5%)
  matrix products  10.1 us (4%)
  other arithmetic  6.46 us (3%)
  blocking collectives  5.94 us (3%)
    pallas_call x1, Pallas kernels, relay(): pl.pallas_call(functools.partial(relay_kernel, split), out_shape=(jax.Sha...  123 us
    pallas_call x1, Pallas kernels, gather_rows(): pl.pallas_call(gather_kernel, out_shape=jax.ShapeDtypeStruct((values.shap...  35.8 us
    pallas_call x2, Pallas kernels, updated_matmul(): pl.pallas_call(updated_matmul_kernel, grid=(steps,), out_shape=jax.ShapeD...  24 us
    pallas_call x1, Pallas kernels, to_rows(): pl.pallas_call(functools.partial(to_rows_kernel, split), out_shape=jax.Sh...  17.8 us
    dot_general x1, matrix products, attend(): jnp.einsum('rsgqd,rlgd->rsgql', queries, key_cache, preferred_element_typ...  6.01 us
    psum x1, blocking collectives, on_device(): lax.psum(partial_out, 'tp').astype(jnp.bfloat16)  5.94 us
    reshape x4, local copies, waits for them, and re-layouts, updated_matmul(): scale = row_scale.reshape(count, steps, depth // BLOCK).transpose(1, 0, 2)  4.89 us

profile of v2, /device:TPU:0, one launch (start us, length us, event | category | flops | bytes accessed | tf_op | source)
XLA Modules:
  0.0 236.4 jit_solution(17901410248495535627)
XLA Ops:
  0.0 0.0 copy-start
  0.0 1.8 reshape.154.hidden
  1.8 1.3 broadcast_in_dim.19.gain
  3.1 123.5 %relay.1 = (bf16[640,5120]{1,0:T(8,128)(2,1)}, bf16[640,4096]{1,0:T(8,128)(2,1)}, bf16[256,5120]{1,0:T(8,128)(2,1)}, f32[8,8,640]{2,1,0:T(8,128)}) custom-call(bf16[5120,640]{1,0:T(8,128)(2,1)} %base.2, bf16[320,8192]{1,0:T(8,128)(2,1)} %codes.2, bf16[256,640]{1,0:T(8,128)(2,1)} %reshape.154.hidden, f32[8,640]{1,0:T(8,128)} %broadcast_in_dim.19.gain), custom_call_target="tpu_custom_call" | custom-call | bytes 250000000 | tf_op jit(solution)/shard_map/relay/pallas_call | solution.py:304
  126.6 0.0 copy-start.2
  126.6 2.5 %fusion.4 = f32[256]{0:T(256)S(1)} fusion(bf16[256,5120]{1,0:T(8,128)(2,1)} %get-tuple-element.9), kind=kLoop, calls=%fused_computation.6 | loop fusion | flops 3931904 | bytes 2622464 | tf_op jit(solution)/shard_map/reduce_sum | solution.py:483
  129.1 0.9 slice.25
  130.0 0.0 copy-done.2
  130.0 2.2 fusion.6.x
  132.3 0.0 copy-done
  132.3 0.4 fusion.21
  132.8 2.5 %copy.38 = f32[640,10,4]{2,0,1:T(8,128)} copy(f32[640,10,4]{0,2,1:T(4,128)S(1)} %reshape.155) | data formatting | bytes 204800 | tf_op jit(solution)/shard_map/reshape | solution.py:433
  135.3 13.2 %updated_matmul.2.values = f32[256,640]{1,0:T(8,128)} custom-call(bf16[256,5120]{1,0:T(8,128)(2,1)} %fusion.6.x, bf16[640,5120]{1,0:T(8,128)(2,1)} %get-tuple-element.11.base, bf16[640,5120]{1,0:T(8,128)(2,1)} %codes.3, f32[10,640,4]{2,1,0:T(8,128)} %bitcast.49), custom_call_target="tpu_custom_call" | custom-call | flops 1677721600 | bytes 13107200 | tf_op jit(solution)/shard_map/updated_matmul/pallas_call | solution.py:434
  148.5 0.0 copy-start.5
  148.5 0.0 copy-start.4
  148.5 0.0 copy-start.6
  148.5 17.8 %to_rows.1 = f32[32,5120]{1,0:T(8,128)} custom-call(f32[256,640]{1,0:T(8,128)} %updated_matmul.2.values), custom_call_target="tpu_custom_call" | custom-call | tf_op jit(solution)/shard_map/to_rows/pallas_call | solution.py:396
  166.3 1.2 reshape_reshape.3
  167.6 0.2 multiply_reduce_fusion.1
  167.7 0.1 copy.44
  167.8 0.1 copy.45
  168.0 0.0 copy-done.5
  168.0 0.1 multiply_multiply_fusion.1
  168.1 0.0 copy-done.4
  168.1 0.1 add_convert_fusion.2
  168.2 0.3 multiply_cosine_fusion
  168.5 0.1 subtract_convert_fusion.1
  168.7 0.3 multiply_reduce_fusion
  168.9 0.1 copy.40
  169.0 0.1 copy.41
  169.2 0.0 copy-done.6
  169.2 0.0 slice-start
  169.2 0.2 multiply_multiply_fusion
  169.4 0.2 subtract_convert_fusion
  169.7 1.4 fusion.42
  171.1 0.1 iota_compare_fusion.4
  171.1 0.0 slice-start.1
  171.1 6.0 %bitcast_reduce_fusion = (f32[16,2,4,8]{3,1,2,0:T(2,128)S(1)}, f32[16,4,2,8,512]{4,3,2,1,0:T(8,128)S(1)}) fusion(pred[16,512]{1,0:T(8,128)(4,1)S(1)} %iota_compare_fusion.4, bf16[16,512,4,128,1]{3,2,1,0,4:T(4,128)(2,1)} %bitcast.51, bf16[16,2,4,8,64]{4,3,1,2,0:T(8,128)(2,1)S(1)} %get-tuple-element.14, bf16[16,2,4,8,64]{4,3,1,2,0:T(8,128)(2,1)S(1)} %get-tuple-element.13), kind=kOutput, calls=%fused_computation.10 | convolution fusion | flops 136313856 | bytes 10760192 | tf_op jit(solution)/shard_map/rsgqd,rlgd->rsgql/dot_general | solution.py:59
  177.2 0.0 slice-done
  177.2 0.0 slice-done.1
  177.2 1.6 fusion.8
  178.8 0.0 copy-start.3
  178.8 0.1 slice.39
  178.9 0.3 fusion.12
  179.2 0.8 convert_element_type.54.values
  180.1 35.8 %gather_rows.1.x = bf16[256,4096]{1,0:T(8,128)(2,1)} custom-call(bf16[32,4096]{1,0:T(8,128)(2,1)} %convert_element_type.54.values), custom_call_target="tpu_custom_call" | custom-call | tf_op jit(solution)/shard_map/gather_rows/pallas_call | solution.py:349
  215.9 0.0 copy-done.3
  216.0 0.4 fusion.22
  216.4 2.3 copy.49
  218.7 0.0 copy-start.1
  218.7 10.8 %updated_matmul.3 = f32[256,640]{1,0:T(8,128)} custom-call(bf16[256,4096]{1,0:T(8,128)(2,1)} %gather_rows.1.x, bf16[640,4096]{1,0:T(8,128)(2,1)} %base.3, bf16[640,4096]{1,0:T(8,128)(2,1)} %get-tuple-element.12.codes, f32[8,640,4]{2,1,0:T(8,128)} %bitcast.50), custom_call_target="tpu_custom_call" | custom-call | flops 1342177280 | bytes 10485760 | tf_op jit(solution)/shard_map/updated_matmul/pallas_call | solution.py:434
  229.6 5.9 %all-reduce.1 = bf16[256,640]{1,0:T(8,128)(2,1)S(1)} all-reduce(f32[256,640]{1,0:T(8,128)} %updated_matmul.3), channel_id=1, replica_groups=mesh['grp'=2,'fsdp'=8,'tp'=2] {'tp'}, use_global_device_ids=true, to_apply=%region_5.6 | all-reduce | flops 163840 | bytes 983040 | tf_op jit(solution)/shard_map/psum | solution.py:499
  235.5 0.8 reshape.157
  236.4 0.0 copy-done.1
  (13 shorter events, 0.2 us)
Async XLA Ops:
  0.0 132.3 %copy-start = (f32[80,40]{0,1:T(8,128)S(1)}, f32[80,40]{0,1:T(8,128)}, u32[]{:S(2)}) copy-start(f32[80,40]{0,1:T(8,128)} %param.19) | copy-start | bytes 38404
  126.6 3.4 %copy-start.2 = (bf16[256,5120]{1,0:T(8,128)(2,1)S(1)}, bf16[256,5120]{1,0:T(8,128)(2,1)}, u32[]{:S(2)}) copy-start(bf16[256,5120]{1,0:T(8,128)(2,1)} %get-tuple-element.9) | copy-start | bytes 7864324
  148.5 19.5 %copy-start.5 = (f32[128]{0:T(128)S(1)}, f32[128]{0:T(128)}, u32[]{:S(2)}) copy-start(f32[128]{0:T(128)} %param.16) | copy-start | bytes 1540
  148.5 19.6 %copy-start.4 = (s32[16]{0:T(128)S(1)}, s32[16]{0:T(128)}, u32[]{:S(2)}) copy-start(s32[16]{0:T(128)} %param.23) | copy-start | bytes 196
  148.5 20.7 %copy-start.6 = (f32[128]{0:T(128)S(1)}, f32[128]{0:T(128)}, u32[]{:S(2)}) copy-start(f32[128]{0:T(128)} %param.15) | copy-start | bytes 1540
  169.2 8.0 %slice-start = ((s8[8388608]{0:T(1024)(128)(4,1)}), s8[4194304]{0:T(1024)(128)(4,1)S(1)}, s32[]{:S(2)}) async-start(s8[8388608]{0:T(1024)(128)(4,1)} %bitcast.53), calls=%async_computation | async-start | bytes 8388608
  171.1 6.1 %slice-start.1 = ((s8[8388608]{0:T(1024)(128)(4,1)}), s8[4194304]{0:T(1024)(128)(4,1)S(1)}, s32[]{:S(2)}) async-start(s8[8388608]{0:T(1024)(128)(4,1)} %bitcast.53), calls=%async_computation.1 | async-start | bytes 8388608
  178.8 37.1 %copy-start.3 = (f32[40,64]{1,0:T(8,128)S(1)}, f32[40,64]{1,0:T(8,128)}, u32[]{:S(2)}) copy-start(f32[40,64]{1,0:T(8,128)} %param.22) | copy-start | bytes 30724
  218.7 17.6 %copy-start.1 = (f32[80,40]{0,1:T(8,128)S(1)}, f32[80,40]{0,1:T(8,128)}, u32[]{:S(2)}) copy-start(f32[80,40]{0,1:T(8,128)} %param.19) | copy-start | bytes 38404

commit v3 on v2

--- a/solution.py
+++ b/solution.py
@@ -191,7 +191,10 @@
 
 
 def chunks_of(rows):
-    return 2 if rows % 32 == 0 else 1
+    return 4 if rows % 64 == 0 else 2 if rows % 32 == 0 else 1
+
+
+WINDOW = 6
 
 
 def relay_kernel(
@@ -224,7 +227,7 @@
         return pl.ds(pl.multiple_of(first + grp * part + chunk * size, 16), size)
 
     started = []
-    base_copies = []
+    plan = []
     hi, lo = fsdp // inner, lax.rem(fsdp, inner)
     for a in range(outer):
         for b in range(inner):
@@ -238,14 +241,17 @@
                     gain, got_gain.at[fsdp], s_gain.at[step], r_gain.at[step], {"fsdp": peer}
                 )
             )
-            for chunk in range(chunks):
-                at = (step, chunk)
-                copy = send(
-                    base.at[my_rows(chunk, peer * rows)],
-                    landing(got_base, split, my_rows(chunk, 0), fsdp, width),
-                    s_base.at[at], r_base.at[at], {"fsdp": peer},
-                )
-                base_copies.append((copy, step, chunk, source))
+            plan += [(step, chunk, peer, source) for chunk in range(chunks)]
+
+    def send_base(step, chunk, peer, source):
+        at = (step, chunk)
+        return send(
+            base.at[my_rows(chunk, peer * rows)],
+            landing(got_base, split, my_rows(chunk, 0), fsdp, width),
+            s_base.at[at], r_base.at[at], {"fsdp": peer},
+        )
+
+    flying = [send_base(*entry) for entry in plan[:WINDOW]]
     own_rows = pl.ds(pl.multiple_of(tp * code_rows, 16), code_rows)
     for step in range(1, halves):
         peer = lax.rem(tp + step, halves)
@@ -272,7 +278,11 @@
     for copy in local:
         copy.start()
     spread.pass_on()
-    for copy, step, chunk, source in base_copies:
+    for index, (step, chunk, _, source) in enumerate(plan):
+        copy = flying[index]
+        copy.wait_send()
+        if index + WINDOW < len(plan):
+            flying.append(send_base(*plan[index + WINDOW]))
         copy.wait_recv()
         block = landing(got_base, split, my_rows(chunk, 0), source, width)
         for hop in range(1, groups):
@@ -283,8 +293,6 @@
                 )
             )
     spread.end()
-    for copy, _, _, _ in base_copies:
-        copy.wait_send()
     for copy in started:
         copy.wait()
     for copy in local:
@@ -307,7 +315,7 @@
             jax.ShapeDtypeStruct(gathered(rows), base.dtype),
             jax.ShapeDtypeStruct((codes.shape[0] * halves, codes.shape[1] // halves), codes.dtype),
             jax.ShapeDtypeStruct(gathered(hidden.shape[0]), hidden.dtype),
-            jax.ShapeDtypeStruct((shards, 8, width), gain.dtype),
+            jax.ShapeDtypeStruct((shards, 1, width), gain.dtype),
         ),
         in_specs=[ANY] * 4,
         out_specs=(ANY,) * 4,
@@ -321,11 +329,11 @@
         compiler_params=pltpu.CompilerParams(collective_id=0, has_side_effects=True),
         cost_estimate=pl.CostEstimate(flops=0, bytes_accessed=250_000_000, transcendentals=0),
         name="relay",
-    )(base, codes, hidden, jnp.broadcast_to(gain[None], (8, width)))
+    )(base, codes, hidden, gain[None])
     if split:
         got_base = jnp.swapaxes(got_base, 0, 1).reshape(rows, shards * width)
         got_hidden = jnp.swapaxes(got_hidden, 0, 1).reshape(-1, shards * width)
-    return got_base, got_codes, got_hidden, got_gain[:, 0].reshape(-1)
+    return got_base, got_codes, got_hidden, got_gain.reshape(-1)
 
 
 def gather_kernel(values, got, s_sem, r_sem, s_local):
@@ -416,21 +424,28 @@
     def _():
         out[...] = jnp.zeros_like(out)
 
-    parts = []
-    for block in range(depth // BLOCK):
-        at = slice(block * BLOCK, (block + 1) * BLOCK)
-        delta = codes[:, at].astype(jnp.float32) * scale[0, :, block : block + 1]
-        parts.append((base[:, at].astype(jnp.float32) + delta).astype(jnp.bfloat16))
+    bands = scale.shape[0]
+    height = base.shape[0] // bands
+    columns = depth // BLOCK
+    first = pl.program_id(0) * columns
+    rows = []
+    for band in range(bands):
+        here = slice(band * height, (band + 1) * height)
+        parts = []
+        for block in range(columns):
+            at = slice(block * BLOCK, (block + 1) * BLOCK)
+            delta = codes[here, at].astype(jnp.float32) * scale[band, first + block]
+            parts.append((base[here, at].astype(jnp.float32) + delta).astype(jnp.bfloat16))
+        rows.append(jnp.concatenate(parts, axis=1))
     out[...] += lax.dot_general(
-        x[...], jnp.concatenate(parts, axis=1), (((1,), (1,)), ((), ())),
+        x[...], jnp.concatenate(rows, axis=0), (((1,), (1,)), ((), ())),
         preferred_element_type=jnp.float32,
     )
 
 
-def updated_matmul(x, base, codes, row_scale, depth=512):
+def updated_matmul(x, base, codes, band_scale, depth=512):
     count, total = base.shape
     steps = total // depth
-    scale = row_scale.reshape(count, steps, depth // BLOCK).transpose(1, 0, 2)
     return pl.pallas_call(
         updated_matmul_kernel,
         grid=(steps,),
@@ -439,7 +454,7 @@
             pl.BlockSpec((x.shape[0], depth), lambda i: (0, i)),
             pl.BlockSpec((count, depth), lambda i: (0, i)),
             pl.BlockSpec((count, depth), lambda i: (0, i)),
-            pl.BlockSpec((1, count, depth // BLOCK), lambda i: (i, 0, 0)),
+            pl.BlockSpec(memory_space=pltpu.SMEM),
         ],
         out_specs=pl.BlockSpec((x.shape[0], count), lambda i: (0, 0)),
         compiler_params=pltpu.CompilerParams(vmem_limit_bytes=56 * 2**20),
@@ -447,11 +462,12 @@
             flops=2 * x.shape[0] * count * total, bytes_accessed=4 * count * total, transcendentals=0
         ),
         name="updated_matmul",
-    )(x, base, codes, scale)
-
-
-def row_scales(scale, first_row, rows):
-    ids = (first_row + jnp.arange(rows, dtype=jnp.int32)) // BLOCK
+    )(x, base, codes, band_scale)
+
+
+def band_scales(scale, first_row, rows):
+    height = math.gcd(rows, BLOCK)
+    ids = (first_row + height * jnp.arange(rows // height, dtype=jnp.int32)) // BLOCK
     pick = (ids[:, None] == jnp.arange(scale.shape[0], dtype=jnp.int32)[None, :]).astype(jnp.float32)
     return jnp.dot(pick, scale, precision=lax.Precision.HIGHEST)
 
@@ -485,7 +501,7 @@
         jnp.bfloat16
     )
     qkv_rows = codes_qkv.shape[0]
-    qkv_scale = row_scales(scale_qkv, (tp_index * shards + fsdp_index) * qkv_rows, qkv_rows)
+    qkv_scale = band_scales(scale_qkv, (tp_index * shards + fsdp_index) * qkv_rows, qkv_rows)
     projected = updated_matmul(normed, arrived_base, codes_qkv, qkv_scale)
     projected = to_rows(projected, shards).reshape(row_count // shards, 2, -1)
     attended = attend(projected, lengths, key_cache, value_cache, q_gain, k_gain)
@@ -493,7 +509,7 @@
     out_rows, out_columns = base_out.shape
     column_blocks = out_columns // BLOCK
     scale_columns = lax.dynamic_slice_in_dim(scale_out, tp_index * column_blocks, column_blocks, 1)
-    out_scale = row_scales(scale_columns, fsdp_index * out_rows, out_rows)
+    out_scale = band_scales(scale_columns, fsdp_index * out_rows, out_rows)
     whole_attended = gather_rows(attended.reshape(-1, attended.shape[-1]), shards)
     partial_out = updated_matmul(whole_attended, base_out, arrived_out, out_scale)
     return lax.psum(partial_out, "tp").astype(jnp.bfloat16).reshape(row_count, 2, out_rows)

time: 237 us -> 227 us (0.958)
  Pallas kernels: 201 us -> 193 us
  local copies, waits for them, and re-layouts: 12.4 us -> 6.59 us
    reshape x4 -> x0, local copies, waits for them, and re-layouts: 4.89 us -> none  [updated_matmul(): scale = row_scale.reshape(count, steps, depth // BLOCK).transpose(1, 0, 2)]
    pallas_call x2, Pallas kernels: 24 us -> 20 us  [updated_matmul(): pl.pallas_call(updated_matmul_kernel, grid=(steps,), out_shape=jax.ShapeD...]
    pallas_call x1, Pallas kernels: 17.8 us -> 14.3 us  [to_rows(): pl.pallas_call(functools.partial(to_rows_kernel, split), out_shape=jax.Sh...]
where the time goes in v3:
time: 227 us; the launch traced here: 225 us
  Pallas kernels  193 us (85%)
  matrix products  10.9 us (5%)
  other arithmetic  8.04 us (4%)
  local copies, waits for them, and re-layouts  6.59 us (3%)
  blocking collectives  5.94 us (3%)
    pallas_call x1, Pallas kernels, relay(): pl.pallas_call(functools.partial(relay_kernel, split), out_shape=(jax.Sha...  124 us
    pallas_call x1, Pallas kernels, gather_rows(): pl.pallas_call(gather_kernel, out_shape=jax.ShapeDtypeStruct((values.shap...  35 us
    pallas_call x2, Pallas kernels, updated_matmul(): pl.pallas_call(updated_matmul_kernel, grid=(steps,), out_shape=jax.ShapeD...  20 us
    pallas_call x1, Pallas kernels, to_rows(): pl.pallas_call(functools.partial(to_rows_kernel, split), out_shape=jax.Sh...  14.3 us
    dot_general x1, matrix products, attend(): jnp.einsum('rsgqd,rlgd->rsgql', queries, key_cache, preferred_element_typ...  6.01 us
    psum x1, blocking collectives, on_device(): lax.psum(partial_out, 'tp').astype(jnp.bfloat16)  5.94 us

profile of v3, /device:TPU:0, one launch (start us, length us, event | category | flops | bytes accessed | tf_op | source)
XLA Modules:
  0.0 224.8 jit_solution(935254850247563215)
XLA Ops:
  0.0 0.0 copy-start
  0.0 1.8 reshape.147.hidden
  1.8 1.3 broadcast_in_dim.19.gain
  3.1 123.7 %relay.1 = (bf16[640,5120]{1,0:T(8,128)(2,1)}, bf16[640,4096]{1,0:T(8,128)(2,1)}, bf16[256,5120]{1,0:T(8,128)(2,1)}, f32[8,1,640]{2,1,0:T(1,128)}) custom-call(bf16[5120,640]{1,0:T(8,128)(2,1)} %base.2, bf16[320,8192]{1,0:T(8,128)(2,1)} %codes.2, bf16[256,640]{1,0:T(8,128)(2,1)} %reshape.147.hidden, f32[1,640]{1,0:T(1,128)} %broadcast_in_dim.19.gain), custom_call_target="tpu_custom_call" | custom-call | bytes 250000000 | tf_op jit(solution)/shard_map/relay/pallas_call | solution.py:312
  126.8 2.3 %fusion.4 = f32[256]{0:T(256)S(1)} fusion(bf16[256,5120]{1,0:T(8,128)(2,1)} %get-tuple-element.9), kind=kLoop, calls=%fused_computation.6 | loop fusion | flops 3931904 | bytes 2622464 | tf_op jit(solution)/shard_map/reduce_sum | solution.py:499
  129.2 4.0 %fusion.6.x = bf16[256,5120]{1,0:T(8,128)(2,1)} fusion(bf16[256,5120]{1,0:T(8,128)(2,1)} %get-tuple-element.9, f32[5120]{0:T(1024)} %bitcast.44, f32[256]{0:T(256)S(1)} %add_rsqrt_fusion.2), kind=kLoop, calls=%fused_computation.8 | loop fusion | flops 5242880 | bytes 5264384 | tf_op jit(solution)/shard_map/convert_element_type | solution.py:500
  133.2 0.0 copy-done
  133.2 0.8 fusion.28.scale
  134.0 0.0 copy-start.3
  134.0 0.0 copy-start.2
  134.0 0.0 copy-start.4
  134.0 11.0 %updated_matmul.2.values = f32[256,640]{1,0:T(8,128)} custom-call(bf16[256,5120]{1,0:T(8,128)(2,1)} %fusion.6.x, bf16[640,5120]{1,0:T(8,128)(2,1)} %get-tuple-element.11.base, bf16[640,5120]{1,0:T(8,128)(2,1)} %codes.3, f32[5,40]{1,0:T(8,128)} %fusion.28.scale), custom_call_target="tpu_custom_call" | custom-call | flops 1677721600 | bytes 13107200 | tf_op jit(solution)/shard_map/updated_matmul/pallas_call | solution.py:449
  145.0 14.3 %to_rows.1 = f32[32,5120]{1,0:T(8,128)} custom-call(f32[256,640]{1,0:T(8,128)} %updated_matmul.2.values), custom_call_target="tpu_custom_call" | custom-call | tf_op jit(solution)/shard_map/to_rows/pallas_call | solution.py:404
  159.3 1.2 reshape_reshape.3
  160.6 0.2 multiply_reduce_fusion.1
  160.7 0.1 copy.39
  160.9 0.1 copy.40
  161.0 0.0 copy-done.3
  161.0 0.1 multiply_multiply_fusion.1
  161.1 0.0 copy-done.2
  161.1 0.1 add_convert_fusion.2
  161.2 0.3 multiply_cosine_fusion
  161.5 0.1 subtract_convert_fusion.1
  161.7 0.3 multiply_reduce_fusion
  161.9 0.1 copy.35
  162.1 0.1 copy.36
  162.2 0.0 copy-done.4
  162.2 0.0 slice-start
  162.2 0.2 multiply_multiply_fusion
  162.4 0.2 subtract_convert_fusion
  162.7 1.4 fusion.36
  164.1 0.1 iota_compare_fusion
  164.2 0.0 slice-start.1
  164.2 6.0 %bitcast_reduce_fusion = (f32[16,2,4,8]{3,1,2,0:T(2,128)S(1)}, f32[16,4,2,8,512]{4,3,2,1,0:T(8,128)S(1)}) fusion(pred[16,512]{1,0:T(8,128)(4,1)S(1)} %iota_compare_fusion, bf16[16,512,4,128,1]{3,2,1,0,4:T(4,128)(2,1)} %bitcast.43, bf16[16,2,4,8,64]{4,3,1,2,0:T(8,128)(2,1)S(1)} %get-tuple-element.14, bf16[16,2,4,8,64]{4,3,1,2,0:T(8,128)(2,1)S(1)} %get-tuple-element.13), kind=kOutput, calls=%fused_computation.10 | convolution fusion | flops 136313856 | bytes 10760192 | tf_op jit(solution)/shard_map/rsgqd,rlgd->rsgql/dot_general | solution.py:59
  170.2 0.0 slice-done
  170.2 0.0 slice-done.1
  170.2 1.6 fusion.8
  171.8 0.0 copy-start.5
  171.8 0.1 slice.35
  171.9 0.3 fusion.12
  172.3 0.8 convert_element_type.54.values
  173.1 35.0 %gather_rows.1.x = bf16[256,4096]{1,0:T(8,128)(2,1)} custom-call(bf16[32,4096]{1,0:T(8,128)(2,1)} %convert_element_type.54.values), custom_call_target="tpu_custom_call" | custom-call | tf_op jit(solution)/shard_map/gather_rows/pallas_call | solution.py:357
  208.1 0.0 copy-done.5
  208.1 0.8 fusion.26.scale
  208.9 0.0 copy-start.1
  208.9 9.0 %updated_matmul.3 = f32[256,640]{1,0:T(8,128)} custom-call(bf16[256,4096]{1,0:T(8,128)(2,1)} %gather_rows.1.x, bf16[640,4096]{1,0:T(8,128)(2,1)} %base.3, bf16[640,4096]{1,0:T(8,128)(2,1)} %get-tuple-element.12.codes, f32[5,32]{1,0:T(8,128)} %fusion.26.scale), custom_call_target="tpu_custom_call" | custom-call | flops 1342177280 | bytes 10485760 | tf_op jit(solution)/shard_map/updated_matmul/pallas_call | solution.py:449
  218.0 5.9 %all-reduce.1 = bf16[256,640]{1,0:T(8,128)(2,1)S(1)} all-reduce(f32[256,640]{1,0:T(8,128)} %updated_matmul.3), channel_id=1, replica_groups=mesh['grp'=2,'fsdp'=8,'tp'=2] {'tp'}, use_global_device_ids=true, to_apply=%region_5.6 | all-reduce | flops 163840 | bytes 983040 | tf_op jit(solution)/shard_map/psum | solution.py:515
  223.9 0.8 reshape.148
  224.8 0.0 copy-done.1
  (11 shorter events, 0.2 us)
Async XLA Ops:
  0.0 133.2 %copy-start = (f32[80,40]{0,1:T(8,128)S(1)}, f32[80,40]{0,1:T(8,128)}, u32[]{:S(2)}) copy-start(f32[80,40]{0,1:T(8,128)} %param.19) | copy-start | bytes 38404
  134.0 27.0 %copy-start.3 = (f32[128]{0:T(128)S(1)}, f32[128]{0:T(128)}, u32[]{:S(2)}) copy-start(f32[128]{0:T(128)} %param.16) | copy-start | bytes 1540
  134.0 27.2 %copy-start.2 = (s32[16]{0:T(128)S(1)}, s32[16]{0:T(128)}, u32[]{:S(2)}) copy-start(s32[16]{0:T(128)} %param.23) | copy-start | bytes 196
  134.0 28.2 %copy-start.4 = (f32[128]{0:T(128)S(1)}, f32[128]{0:T(128)}, u32[]{:S(2)}) copy-start(f32[128]{0:T(128)} %param.15) | copy-start | bytes 1540
  162.2 8.0 %slice-start = ((s8[8388608]{0:T(1024)(128)(4,1)}), s8[4194304]{0:T(1024)(128)(4,1)S(1)}, s32[]{:S(2)}) async-start(s8[8388608]{0:T(1024)(128)(4,1)} %bitcast.45), calls=%async_computation | async-start | bytes 8388608
  164.2 6.1 %slice-start.1 = ((s8[8388608]{0:T(1024)(128)(4,1)}), s8[4194304]{0:T(1024)(128)(4,1)S(1)}, s32[]{:S(2)}) async-start(s8[8388608]{0:T(1024)(128)(4,1)} %bitcast.45), calls=%async_computation.1 | async-start | bytes 8388608
  171.8 36.3 %copy-start.5 = (f32[40,64]{1,0:T(8,128)S(1)}, f32[40,64]{1,0:T(8,128)}, u32[]{:S(2)}) copy-start(f32[40,64]{1,0:T(8,128)} %param.22) | copy-start | bytes 30724
  208.9 15.8 %copy-start.1 = (f32[80,40]{0,1:T(8,128)S(1)}, f32[80,40]{0,1:T(8,128)}, u32[]{:S(2)}) copy-start(f32[80,40]{0,1:T(8,128)} %param.19) | copy-start | bytes 38404

commit v4 on v3

--- a/solution.py
+++ b/solution.py
@@ -173,11 +173,17 @@
             )
 
     def pass_on(self):
+        self.pass_outer()
+        self.pass_inner()
+
+    def pass_outer(self):
         for a in range(1, self.outer):
             self.arriving[a, 0].wait_recv()
             source = lax.rem(self.hi + self.outer - a, self.outer) * self.inner + self.lo
             self.inward(a, self.place(source))
             self.across(a, 0)
+
+    def pass_inner(self):
         for a in range(self.outer):
             for b in range(1, self.inner):
                 self.arriving[a, b].wait_recv()
@@ -338,28 +344,47 @@
 
 def gather_kernel(values, got, s_sem, r_sem, s_local):
     rows = values.shape[0]
+    chunks = s_sem.shape[0]
+    size = values.shape[1] // chunks
     greet(("fsdp",))
 
-    def place(source):
-        return got.at[pl.ds(pl.multiple_of(source * rows, 16), rows)]
-
-    spread = Spread(values, place, (s_sem, r_sem, None, None), False)
-    spread.begin()
+    def place(source, columns=slice(None)):
+        return got.at[pl.ds(pl.multiple_of(source * rows, 16), rows), columns]
+
+    spreads = []
+    for chunk in range(chunks):
+        columns = pl.ds(chunk * size, size)
+        spreads.append(
+            Spread(
+                values.at[:, columns],
+                functools.partial(place, columns=columns),
+                (s_sem.at[chunk], r_sem.at[chunk], None, None),
+                False,
+            )
+        )
+    for spread in spreads[:2]:
+        spread.begin()
     local = pltpu.make_async_copy(values, place(lax.axis_index("fsdp")), s_local)
     local.start()
-    spread.pass_on()
-    spread.end()
+    for chunk, spread in enumerate(spreads):
+        spread.pass_outer()
+        if chunk + 2 < chunks:
+            spreads[chunk + 2].begin()
+    for spread in spreads:
+        spread.pass_inner()
+        spread.end()
     local.wait()
 
 
 def gather_rows(values, shards):
+    chunks = 4 if values.shape[1] % 512 == 0 else 1
     dma = pltpu.SemaphoreType.DMA
     return pl.pallas_call(
         gather_kernel,
         out_shape=jax.ShapeDtypeStruct((values.shape[0] * shards, values.shape[1]), values.dtype),
         in_specs=[ANY],
         out_specs=ANY,
-        scratch_shapes=[dma((shards,)), dma((shards,)), dma],
+        scratch_shapes=[dma((chunks, shards)), dma((chunks, shards)), dma],
         compiler_params=pltpu.CompilerParams(collective_id=2, has_side_effects=True),
         name="gather_rows",
     )(values)

time: 227 us -> 224 us (0.987)
  no operation moved by 1% of the time
where the time goes in v4:
time: 224 us; the launch traced here: 223 us
  Pallas kernels  192 us (86%)
  matrix products  10.9 us (5%)
  other arithmetic  8.04 us (4%)
  local copies, waits for them, and re-layouts  6.59 us (3%)
  blocking collectives  5.94 us (3%)
    pallas_call x1, Pallas kernels, relay(): pl.pallas_call(functools.partial(relay_kernel, split), out_shape=(jax.Sha...  124 us
    pallas_call x1, Pallas kernels, gather_rows(): pl.pallas_call(gather_kernel, out_shape=jax.ShapeDtypeStruct((values.shap...  33.7 us
    pallas_call x2, Pallas kernels, updated_matmul(): pl.pallas_call(updated_matmul_kernel, grid=(steps,), out_shape=jax.ShapeD...  20 us
    pallas_call x1, Pallas kernels, to_rows(): pl.pallas_call(functools.partial(to_rows_kernel, split), out_shape=jax.Sh...  14.3 us
    dot_general x1, matrix products, attend(): jnp.einsum('rsgqd,rlgd->rsgql', queries, key_cache, preferred_element_typ...  6.01 us
    psum x1, blocking collectives, on_device(): lax.psum(partial_out, 'tp').astype(jnp.bfloat16)  5.94 us

profile of v4, /device:TPU:0, one launch (start us, length us, event | category | flops | bytes accessed | tf_op | source)
XLA Modules:
  0.0 223.5 jit_solution(11795846081959427253)
XLA Ops:
  0.0 0.0 copy-start
  0.0 1.8 reshape.147.hidden
  1.8 1.3 broadcast_in_dim.19.gain
  3.1 123.7 %relay.1 = (bf16[640,5120]{1,0:T(8,128)(2,1)}, bf16[640,4096]{1,0:T(8,128)(2,1)}, bf16[256,5120]{1,0:T(8,128)(2,1)}, f32[8,1,640]{2,1,0:T(1,128)}) custom-call(bf16[5120,640]{1,0:T(8,128)(2,1)} %base.2, bf16[320,8192]{1,0:T(8,128)(2,1)} %codes.2, bf16[256,640]{1,0:T(8,128)(2,1)} %reshape.147.hidden, f32[1,640]{1,0:T(1,128)} %broadcast_in_dim.19.gain), custom_call_target="tpu_custom_call" | custom-call | bytes 250000000 | tf_op jit(solution)/shard_map/relay/pallas_call | solution.py:318
  126.8 2.3 %fusion.4 = f32[256]{0:T(256)S(1)} fusion(bf16[256,5120]{1,0:T(8,128)(2,1)} %get-tuple-element.9), kind=kLoop, calls=%fused_computation.6 | loop fusion | flops 3931904 | bytes 2622464 | tf_op jit(solution)/shard_map/reduce_sum | solution.py:524
  129.2 4.0 %fusion.6.x = bf16[256,5120]{1,0:T(8,128)(2,1)} fusion(bf16[256,5120]{1,0:T(8,128)(2,1)} %get-tuple-element.9, f32[5120]{0:T(1024)} %bitcast.44, f32[256]{0:T(256)S(1)} %add_rsqrt_fusion.2), kind=kLoop, calls=%fused_computation.8 | loop fusion | flops 5242880 | bytes 5264384 | tf_op jit(solution)/shard_map/convert_element_type | solution.py:525
  133.2 0.0 copy-done
  133.2 0.8 fusion.28.scale
  134.0 0.0 copy-start.3
  134.0 0.0 copy-start.2
  134.0 0.0 copy-start.4
  134.0 11.0 %updated_matmul.2.values = f32[256,640]{1,0:T(8,128)} custom-call(bf16[256,5120]{1,0:T(8,128)(2,1)} %fusion.6.x, bf16[640,5120]{1,0:T(8,128)(2,1)} %get-tuple-element.11.base, bf16[640,5120]{1,0:T(8,128)(2,1)} %codes.3, f32[5,40]{1,0:T(8,128)} %fusion.28.scale), custom_call_target="tpu_custom_call" | custom-call | flops 1677721600 | bytes 13107200 | tf_op jit(solution)/shard_map/updated_matmul/pallas_call | solution.py:474
  145.0 14.3 %to_rows.1 = f32[32,5120]{1,0:T(8,128)} custom-call(f32[256,640]{1,0:T(8,128)} %updated_matmul.2.values), custom_call_target="tpu_custom_call" | custom-call | tf_op jit(solution)/shard_map/to_rows/pallas_call | solution.py:429
  159.3 1.2 reshape_reshape.3
  160.6 0.2 multiply_reduce_fusion.1
  160.7 0.1 copy.39
  160.9 0.1 copy.40
  161.0 0.0 copy-done.3
  161.0 0.1 multiply_multiply_fusion.1
  161.1 0.0 copy-done.2
  161.1 0.1 add_convert_fusion.2
  161.2 0.3 multiply_cosine_fusion
  161.5 0.1 subtract_convert_fusion.1
  161.7 0.3 multiply_reduce_fusion
  161.9 0.1 copy.35
  162.1 0.1 copy.36
  162.2 0.0 copy-done.4
  162.2 0.0 slice-start
  162.2 0.2 multiply_multiply_fusion
  162.4 0.2 subtract_convert_fusion
  162.7 1.4 fusion.36
  164.1 0.1 iota_compare_fusion
  164.2 0.0 slice-start.1
  164.2 6.0 %bitcast_reduce_fusion = (f32[16,2,4,8]{3,1,2,0:T(2,128)S(1)}, f32[16,4,2,8,512]{4,3,2,1,0:T(8,128)S(1)}) fusion(pred[16,512]{1,0:T(8,128)(4,1)S(1)} %iota_compare_fusion, bf16[16,512,4,128,1]{3,2,1,0,4:T(4,128)(2,1)} %bitcast.43, bf16[16,2,4,8,64]{4,3,1,2,0:T(8,128)(2,1)S(1)} %get-tuple-element.14, bf16[16,2,4,8,64]{4,3,1,2,0:T(8,128)(2,1)S(1)} %get-tuple-element.13), kind=kOutput, calls=%fused_computation.10 | convolution fusion | flops 136313856 | bytes 10760192 | tf_op jit(solution)/shard_map/rsgqd,rlgd->rsgql/dot_general | solution.py:59
  170.2 0.0 slice-done
  170.2 0.0 slice-done.1
  170.2 1.6 fusion.8
  171.8 0.0 copy-start.5
  171.8 0.1 slice.35
  171.9 0.3 fusion.12
  172.3 0.8 convert_element_type.54.values
  173.1 33.7 %gather_rows.1.x = bf16[256,4096]{1,0:T(8,128)(2,1)} custom-call(bf16[32,4096]{1,0:T(8,128)(2,1)} %convert_element_type.54.values), custom_call_target="tpu_custom_call" | custom-call | tf_op jit(solution)/shard_map/gather_rows/pallas_call | solution.py:382
  206.8 0.0 copy-done.5
  206.8 0.8 fusion.26.scale
  207.6 0.0 copy-start.1
  207.6 9.0 %updated_matmul.3 = f32[256,640]{1,0:T(8,128)} custom-call(bf16[256,4096]{1,0:T(8,128)(2,1)} %gather_rows.1.x, bf16[640,4096]{1,0:T(8,128)(2,1)} %base.3, bf16[640,4096]{1,0:T(8,128)(2,1)} %get-tuple-element.12.codes, f32[5,32]{1,0:T(8,128)} %fusion.26.scale), custom_call_target="tpu_custom_call" | custom-call | flops 1342177280 | bytes 10485760 | tf_op jit(solution)/shard_map/updated_matmul/pallas_call | solution.py:474
  216.7 5.9 %all-reduce.1 = bf16[256,640]{1,0:T(8,128)(2,1)S(1)} all-reduce(f32[256,640]{1,0:T(8,128)} %updated_matmul.3), channel_id=1, replica_groups=mesh['grp'=2,'fsdp'=8,'tp'=2] {'tp'}, use_global_device_ids=true, to_apply=%region_5.6 | all-reduce | flops 163840 | bytes 983040 | tf_op jit(solution)/shard_map/psum | solution.py:540
  222.6 0.8 reshape.148
  223.5 0.0 copy-done.1
  (11 shorter events, 0.2 us)
Async XLA Ops:
  0.0 133.2 %copy-start = (f32[80,40]{0,1:T(8,128)S(1)}, f32[80,40]{0,1:T(8,128)}, u32[]{:S(2)}) copy-start(f32[80,40]{0,1:T(8,128)} %param.19) | copy-start | bytes 38404
  134.0 27.0 %copy-start.3 = (f32[128]{0:T(128)S(1)}, f32[128]{0:T(128)}, u32[]{:S(2)}) copy-start(f32[128]{0:T(128)} %param.16) | copy-start | bytes 1540
  134.0 27.2 %copy-start.2 = (s32[16]{0:T(128)S(1)}, s32[16]{0:T(128)}, u32[]{:S(2)}) copy-start(s32[16]{0:T(128)} %param.23) | copy-start | bytes 196
  134.0 28.2 %copy-start.4 = (f32[128]{0:T(128)S(1)}, f32[128]{0:T(128)}, u32[]{:S(2)}) copy-start(f32[128]{0:T(128)} %param.15) | copy-start | bytes 1540
  162.2 8.0 %slice-start = ((s8[8388608]{0:T(1024)(128)(4,1)}), s8[4194304]{0:T(1024)(128)(4,1)S(1)}, s32[]{:S(2)}) async-start(s8[8388608]{0:T(1024)(128)(4,1)} %bitcast.45), calls=%async_computation | async-start | bytes 8388608
  164.2 6.1 %slice-start.1 = ((s8[8388608]{0:T(1024)(128)(4,1)}), s8[4194304]{0:T(1024)(128)(4,1)S(1)}, s32[]{:S(2)}) async-start(s8[8388608]{0:T(1024)(128)(4,1)} %bitcast.45), calls=%async_computation.1 | async-start | bytes 8388608
  171.8 35.0 %copy-start.5 = (f32[40,64]{1,0:T(8,128)S(1)}, f32[40,64]{1,0:T(8,128)}, u32[]{:S(2)}) copy-start(f32[40,64]{1,0:T(8,128)} %param.22) | copy-start | bytes 30724
  207.6 15.8 %copy-start.1 = (f32[80,40]{0,1:T(8,128)S(1)}, f32[80,40]{0,1:T(8,128)}, u32[]{:S(2)}) copy-start(f32[80,40]{0,1:T(8,128)} %param.19) | copy-start | bytes 38404

commit v5 on v4

--- a/solution.py
+++ b/solution.py
@@ -200,7 +200,7 @@
     return 4 if rows % 64 == 0 else 2 if rows % 32 == 0 else 1
 
 
-WINDOW = 6
+WINDOW = 14
 
 
 def relay_kernel(

time: 224 us -> 227 us (1.013)
  Pallas kernels: 192 us -> 195 us
    pallas_call x1, Pallas kernels: 14.3 us -> 16.7 us  [to_rows(): pl.pallas_call(functools.partial(to_rows_kernel, split), out_shape=jax.Sh...]
where the time goes in v5:
time: 227 us
  Pallas kernels  195 us (86%)
  matrix products  10.9 us (5%)
  other arithmetic  8.04 us (4%)
  local copies, waits for them, and re-layouts  6.59 us (3%)
  blocking collectives  5.94 us (3%)
    pallas_call x1, Pallas kernels, relay(): pl.pallas_call(functools.partial(relay_kernel, split), out_shape=(jax.Sha...  124 us
    pallas_call x1, Pallas kernels, gather_rows(): pl.pallas_call(gather_kernel, out_shape=jax.ShapeDtypeStruct((values.shap...  34.6 us
    pallas_call x2, Pallas kernels, updated_matmul(): pl.pallas_call(updated_matmul_kernel, grid=(steps,), out_shape=jax.ShapeD...  20 us
    pallas_call x1, Pallas kernels, to_rows(): pl.pallas_call(functools.partial(to_rows_kernel, split), out_shape=jax.Sh...  16.7 us
    dot_general x1, matrix products, attend(): jnp.einsum('rsgqd,rlgd->rsgql', queries, key_cache, preferred_element_typ...  6.01 us
    psum x1, blocking collectives, on_device(): lax.psum(partial_out, 'tp').astype(jnp.bfloat16)  5.94 us

profile of v5, /device:TPU:0, one launch (start us, length us, event | category | flops | bytes accessed | tf_op | source)
XLA Modules:
  0.0 226.8 jit_solution(16085449147134912263)
XLA Ops:
  0.0 0.0 copy-start
  0.0 1.8 reshape.147.hidden
  1.8 1.3 broadcast_in_dim.19.gain
  3.1 123.8 %relay.1 = (bf16[640,5120]{1,0:T(8,128)(2,1)}, bf16[640,4096]{1,0:T(8,128)(2,1)}, bf16[256,5120]{1,0:T(8,128)(2,1)}, f32[8,1,640]{2,1,0:T(1,128)}) custom-call(bf16[5120,640]{1,0:T(8,128)(2,1)} %base.2, bf16[320,8192]{1,0:T(8,128)(2,1)} %codes.2, bf16[256,640]{1,0:T(8,128)(2,1)} %reshape.147.hidden, f32[1,640]{1,0:T(1,128)} %broadcast_in_dim.19.gain), custom_call_target="tpu_custom_call" | custom-call | bytes 250000000 | tf_op jit(solution)/shard_map/relay/pallas_call | solution.py:318
  126.9 2.3 %fusion.4 = f32[256]{0:T(256)S(1)} fusion(bf16[256,5120]{1,0:T(8,128)(2,1)} %get-tuple-element.9), kind=kLoop, calls=%fused_computation.6 | loop fusion | flops 3931904 | bytes 2622464 | tf_op jit(solution)/shard_map/reduce_sum | solution.py:524
  129.2 4.0 %fusion.6.x = bf16[256,5120]{1,0:T(8,128)(2,1)} fusion(bf16[256,5120]{1,0:T(8,128)(2,1)} %get-tuple-element.9, f32[5120]{0:T(1024)} %bitcast.44, f32[256]{0:T(256)S(1)} %add_rsqrt_fusion.2), kind=kLoop, calls=%fused_computation.8 | loop fusion | flops 5242880 | bytes 5264384 | tf_op jit(solution)/shard_map/convert_element_type | solution.py:525
  133.2 0.0 copy-done
  133.2 0.8 fusion.28.scale
  134.0 0.0 copy-start.3
  134.0 0.0 copy-start.2
  134.0 0.0 copy-start.4
  134.0 11.0 %updated_matmul.2.values = f32[256,640]{1,0:T(8,128)} custom-call(bf16[256,5120]{1,0:T(8,128)(2,1)} %fusion.6.x, bf16[640,5120]{1,0:T(8,128)(2,1)} %get-tuple-element.11.base, bf16[640,5120]{1,0:T(8,128)(2,1)} %codes.3, f32[5,40]{1,0:T(8,128)} %fusion.28.scale), custom_call_target="tpu_custom_call" | custom-call | flops 1677721600 | bytes 13107200 | tf_op jit(solution)/shard_map/updated_matmul/pallas_call | solution.py:474
  145.0 16.7 %to_rows.1 = f32[32,5120]{1,0:T(8,128)} custom-call(f32[256,640]{1,0:T(8,128)} %updated_matmul.2.values), custom_call_target="tpu_custom_call" | custom-call | tf_op jit(solution)/shard_map/to_rows/pallas_call | solution.py:429
  161.7 1.2 reshape_reshape.3
  163.0 0.2 multiply_reduce_fusion.1
  163.2 0.1 copy.39
  163.3 0.1 copy.40
  163.4 0.0 copy-done.3
  163.4 0.1 multiply_multiply_fusion.1
  163.6 0.0 copy-done.2
  163.6 0.1 add_convert_fusion.2
  163.6 0.3 multiply_cosine_fusion
  164.0 0.1 subtract_convert_fusion.1
  164.1 0.3 multiply_reduce_fusion
  164.4 0.1 copy.35
  164.5 0.1 copy.36
  164.6 0.0 copy-done.4
  164.6 0.0 slice-start
  164.6 0.2 multiply_multiply_fusion
  164.8 0.2 subtract_convert_fusion
  165.1 1.4 fusion.36
  166.5 0.1 iota_compare_fusion
  166.6 0.0 slice-start.1
  166.6 6.0 %bitcast_reduce_fusion = (f32[16,2,4,8]{3,1,2,0:T(2,128)S(1)}, f32[16,4,2,8,512]{4,3,2,1,0:T(8,128)S(1)}) fusion(pred[16,512]{1,0:T(8,128)(4,1)S(1)} %iota_compare_fusion, bf16[16,512,4,128,1]{3,2,1,0,4:T(4,128)(2,1)} %bitcast.43, bf16[16,2,4,8,64]{4,3,1,2,0:T(8,128)(2,1)S(1)} %get-tuple-element.14, bf16[16,2,4,8,64]{4,3,1,2,0:T(8,128)(2,1)S(1)} %get-tuple-element.13), kind=kOutput, calls=%fused_computation.10 | convolution fusion | flops 136313856 | bytes 10760192 | tf_op jit(solution)/shard_map/rsgqd,rlgd->rsgql/dot_general | solution.py:59
  172.6 0.0 slice-done
  172.7 0.0 slice-done.1
  172.7 1.6 fusion.8
  174.3 0.0 copy-start.5
  174.3 0.1 slice.35
  174.3 0.3 fusion.12
  174.7 0.8 convert_element_type.54.values
  175.5 34.6 %gather_rows.1.x = bf16[256,4096]{1,0:T(8,128)(2,1)} custom-call(bf16[32,4096]{1,0:T(8,128)(2,1)} %convert_element_type.54.values), custom_call_target="tpu_custom_call" | custom-call | tf_op jit(solution)/shard_map/gather_rows/pallas_call | solution.py:382
  210.1 0.0 copy-done.5
  210.1 0.8 fusion.26.scale
  210.9 0.0 copy-start.1
  210.9 9.0 %updated_matmul.3 = f32[256,640]{1,0:T(8,128)} custom-call(bf16[256,4096]{1,0:T(8,128)(2,1)} %gather_rows.1.x, bf16[640,4096]{1,0:T(8,128)(2,1)} %base.3, bf16[640,4096]{1,0:T(8,128)(2,1)} %get-tuple-element.12.codes, f32[5,32]{1,0:T(8,128)} %fusion.26.scale), custom_call_target="tpu_custom_call" | custom-call | flops 1342177280 | bytes 10485760 | tf_op jit(solution)/shard_map/updated_matmul/pallas_call | solution.py:474
  220.0 5.9 %all-reduce.1 = bf16[256,640]{1,0:T(8,128)(2,1)S(1)} all-reduce(f32[256,640]{1,0:T(8,128)} %updated_matmul.3), channel_id=1, replica_groups=mesh['grp'=2,'fsdp'=8,'tp'=2] {'tp'}, use_global_device_ids=true, to_apply=%region_5.6 | all-reduce | flops 163840 | bytes 983040 | tf_op jit(solution)/shard_map/psum | solution.py:540
  225.9 0.8 reshape.148
  226.8 0.0 copy-done.1
  (11 shorter events, 0.2 us)
Async XLA Ops:
  0.0 133.2 %copy-start = (f32[80,40]{0,1:T(8,128)S(1)}, f32[80,40]{0,1:T(8,128)}, u32[]{:S(2)}) copy-start(f32[80,40]{0,1:T(8,128)} %param.19) | copy-start | bytes 38404
  134.0 29.4 %copy-start.3 = (f32[128]{0:T(128)S(1)}, f32[128]{0:T(128)}, u32[]{:S(2)}) copy-start(f32[128]{0:T(128)} %param.16) | copy-start | bytes 1540
  134.0 29.5 %copy-start.2 = (s32[16]{0:T(128)S(1)}, s32[16]{0:T(128)}, u32[]{:S(2)}) copy-start(s32[16]{0:T(128)} %param.23) | copy-start | bytes 196
  134.0 30.6 %copy-start.4 = (f32[128]{0:T(128)S(1)}, f32[128]{0:T(128)}, u32[]{:S(2)}) copy-start(f32[128]{0:T(128)} %param.15) | copy-start | bytes 1540
  164.6 8.0 %slice-start = ((s8[8388608]{0:T(1024)(128)(4,1)}), s8[4194304]{0:T(1024)(128)(4,1)S(1)}, s32[]{:S(2)}) async-start(s8[8388608]{0:T(1024)(128)(4,1)} %bitcast.45), calls=%async_computation | async-start | bytes 8388608
  166.6 6.1 %slice-start.1 = ((s8[8388608]{0:T(1024)(128)(4,1)}), s8[4194304]{0:T(1024)(128)(4,1)S(1)}, s32[]{:S(2)}) async-start(s8[8388608]{0:T(1024)(128)(4,1)} %bitcast.45), calls=%async_computation.1 | async-start | bytes 8388608
  174.3 35.9 %copy-start.5 = (f32[40,64]{1,0:T(8,128)S(1)}, f32[40,64]{1,0:T(8,128)}, u32[]{:S(2)}) copy-start(f32[40,64]{1,0:T(8,128)} %param.22) | copy-start | bytes 30724
  210.9 15.8 %copy-start.1 = (f32[80,40]{0,1:T(8,128)S(1)}, f32[80,40]{0,1:T(8,128)}, u32[]{:S(2)}) copy-start(f32[80,40]{0,1:T(8,128)} %param.19) | copy-start | bytes 38404
